TPU v7x, 512 devices: a whole 4x4x16 slice. The times are simulated.
512 devices in a mesh: feed: 8 (over y, z_hi), tm: 64 (over x, z_lo, core).
Axes of the slice: x: 4, y: 4, z: 16 (z_hi: 2, z_lo: 8; z = z_hi * 8 + z_lo), core: 2. Of those that a mesh axis runs over, the one named last changes fastest.
Arguments:
- voltages: bfloat16 [256, 524288], P('feed', 'tm'), may hold values from -6 to 6
- previous: bfloat16 [256, 30720], P('feed'), may hold values from -16 to 16
- filter_taps: float32 [16, 2048], replicated, may hold values from -1 to 1
Outputs:
- visibilities: float32 [2, 1024, 256, 256], P(None, 'tm', 'feed')
All inputs are finite; a program needn't handle non-finite values.
Results may differ from a plain program's by a relative error of at most 0.0095.
Values may be sent and summed in bfloat16 or wider, within the bound.
No kernel may reach another device: no remote copies, remote signals or barrier semaphores. Data moves between devices by JAX's collectives and lax.ppermute only.
A program may use at most 64 MiB of HBM per device.

v0:
```python
import math

import jax
import jax.numpy as jnp
from jax import lax
from jax.sharding import PartitionSpec as P


def shifted(block, axis, distance):
    devices = range(lax.axis_size(axis))
    route = [(i - distance, i) for i in devices if i - distance in devices]
    return lax.ppermute(block, axis, route)


def correlate(first_set, second_set):
    real_sum = jnp.einsum(
        "ctas,ctbs->cab", first_set[0], second_set[0], preferred_element_type=jnp.float32
    )
    real_sum = real_sum + jnp.einsum(
        "ctas,ctbs->cab", first_set[1], second_set[1], preferred_element_type=jnp.float32
    )
    imag_sum = jnp.einsum(
        "ctas,ctbs->cab", first_set[1], second_set[0], preferred_element_type=jnp.float32
    )
    imag_sum = imag_sum - jnp.einsum(
        "ctas,ctbs->cab", first_set[0], second_set[1], preferred_element_type=jnp.float32
    )
    return (real_sum, imag_sum)


def body(voltages, previous, filter_taps):
    inputs_here, sample_count = voltages.shape
    tap_count, frame_len = filter_taps.shape
    spectra_here = sample_count // frame_len
    reach_frames = tap_count - 1
    current = voltages.reshape(inputs_here, spectra_here, frame_len)
    count_back = (reach_frames + spectra_here - 1) // spectra_here
    arrivals = []
    for distance in range(count_back, 0, -1):
        frame_count = min(spectra_here, reach_frames - (distance - 1) * spectra_here)
        arrivals.append(shifted(current[:, spectra_here - frame_count :, :], "tm", distance))
    preceding = jnp.concatenate(arrivals, axis=1)
    first_frame = lax.axis_index("tm") * spectra_here
    history_frames = previous.reshape(inputs_here, reach_frames, frame_len)
    padded = jnp.concatenate([history_frames, jnp.zeros_like(history_frames)], axis=1)
    start_frame = jnp.minimum(first_frame, reach_frames)
    from_history = lax.dynamic_slice_in_dim(padded, start_frame, reach_frames, 1)
    frame_index = lax.broadcasted_iota(jnp.int32, (1, reach_frames, 1), 1)
    preceding = jnp.where(frame_index < reach_frames - first_frame, from_history, preceding)
    extended = jnp.concatenate([preceding, current], axis=1)
    filtered = jnp.zeros((inputs_here, spectra_here, frame_len), jnp.float32)
    for tap_index in range(tap_count):
        filtered = filtered + filter_taps[tap_index] * extended[
            :, tap_index : tap_index + spectra_here
        ].astype(jnp.float32)
    frame_rows = filtered.astype(jnp.bfloat16).reshape(inputs_here * spectra_here, frame_len)
    half_len = frame_len // 2
    sample_index = lax.broadcasted_iota(jnp.int32, (frame_len, 2 * half_len), 0)
    column_index = lax.broadcasted_iota(jnp.int32, (frame_len, 2 * half_len), 1)
    channel_index = column_index % half_len
    angle = (sample_index * channel_index % frame_len).astype(jnp.float32) * (
        2.0 * math.pi / frame_len
    )
    table = jnp.where(column_index < half_len, jnp.cos(angle), -jnp.sin(angle))
    table_high = table.astype(jnp.bfloat16)
    table_low = (table - table_high.astype(jnp.float32)).astype(jnp.bfloat16)
    scaling = 1.0 / math.sqrt(frame_len)
    transformed = jnp.einsum(
        "rn,nk->kr", frame_rows, table_high, preferred_element_type=jnp.float32
    )
    transformed = transformed + jnp.einsum(
        "rn,nk->kr", frame_rows, table_low, preferred_element_type=jnp.float32
    )
    spectra_pair = (
        (transformed * scaling)
        .reshape(2, half_len, inputs_here * spectra_here)
        .astype(jnp.bfloat16)
    )
    turned = lax.all_to_all(spectra_pair, "tm", split_axis=1, concat_axis=2, tiled=True)
    time_devices = lax.axis_size("tm")
    channels_here = turned.shape[1]
    spectra_blocks = turned.reshape(2, channels_here, time_devices, inputs_here, spectra_here)
    average = 1.0 / (time_devices * spectra_here)
    real_sum, imag_sum = correlate(
        spectra_blocks, lax.all_gather(spectra_blocks, "feed", axis=3, tiled=True)
    )
    visibility = jnp.stack([real_sum, imag_sum])
    return visibility * average


def solution(mesh):
    placed = (P("feed", "tm"), P("feed", None), P())
    return jax.shard_map(
        body, mesh=mesh, in_specs=placed, out_specs=P(None, "tm", "feed", None), check_vma=False
    )
```

profile of v0, /device:TPU:98, one launch (start us, length us, event | category | flops | bytes accessed | tf_op | source)
XLA Modules:
  0.0 594.3 jit_solution(7218386997453825720)
XLA Ops:
  6.5 1.4 reshape.41
  8.0 4.5 collective-permute-start.1
  12.5 3.8 collective-permute-start.2
  16.3 3.7 collective-permute-start.3
  20.0 0.3 slice.150
  20.3 3.6 collective-permute-start
  23.9 3.2 reshape.40
  27.1 1.7 fusion.68
  28.8 33.1 %collective-permute-done = bf16[32,3,2048]{2,1,0:T(4,128)(2,1)} collective-permute-done((bf16[32,3,2048]{2,1,0:T(4,128)(2,1)S(1)}, bf16[32,3,2048]{2,1,0:T(4,128)(2,1)}, u32[]{:S(2)}, u32[]{:S(2)}) %collective-permute-start) | collective-permute-done | bytes 393248 | tf_op jit(solution)/shard_map/ppermute | solution.py:12
  61.9 0.0 collective-permute-done.1
  61.9 3.7 fusion.17
  65.6 5.1 add_convert_fusion
  70.7 0.1 reshape.42
  70.8 69.2 %fusion.3 = f32[2048,128]{1,0:T(8,128)S(1)} fusion(bf16[128,2048]{1,0:T(8,128)(2,1)S(1)} %reshape.42, s32[2048]{0:T(1024)S(1)} %iota_and_fusion, s32[2048]{0:T(1024)S(1)} %fusion.54, pred[2048]{0:T(1024)(128)(4,1)S(1)} %get-tuple-element.26, pred[2048]{0:T(1024)(128)(4,1)S(1)} %get-tuple-element.25), kind=kOutput, calls=%fused_computation.8 | convolution fusion | flops 1161822208 | bytes 1593344 | tf_op jit(solution)/shard_map/rn,nk->kr/dot_general | solution.py:71
  140.0 68.5 %fusion.14 = bf16[2048,128]{1,0:T(8,128)(2,1)S(1)} fusion(f32[2048,128]{1,0:T(8,128)S(1)} %fusion.3, bf16[128,2048]{1,0:T(8,128)(2,1)S(1)} %reshape.42, s32[2048]{0:T(1024)S(1)} %iota_and_fusion, s32[2048]{0:T(1024)S(1)} %fusion.54, pred[2048]{0:T(1024)(128)(4,1)S(1)} %get-tuple-element.26, pred[2048]{0:T(1024)(128)(4,1)S(1)} %get-tuple-element.25), kind=kOutput, calls=%fused_computation.14 | convolution fusion | flops 1150025728 | bytes 2117632 | tf_op jit(solution)/shard_map/rn,nk->kr/dot_general | solution.py:68
  208.6 0.5 copy.17
  209.1 48.0 %all_to_all.15 = bf16[2,1024,128]{2,0,1:T(2,128)(2,1)S(1)} all-to-all(bf16[2,1024,128]{2,0,1:T(2,128)(2,1)S(1)} %copy.17), channel_id=1, replica_groups=mesh['feed'=8,'tm'=64] {'tm'}, dimensions={1} | all-to-all | bytes 1048576 | tf_op jit(solution)/shard_map/all_to_all | solution.py:79
  257.2 0.1 copy.18
  257.2 1.1 copy.20
  258.3 1.2 copy.21
  259.5 0.0 all-gather.2.cloned.1.call-update
  259.6 0.5 copy.19
  260.1 0.5 copy.24
  260.7 302.3 %all-gather.2.cloned.1.call-done = bf16[2,16,64,256,4]{2,1,4,0,3:T(8,128)(2,1)} async-done(((bf16[2,16,64,32,4]{2,1,4,0,3:T(8,128)(2,1)}), bf16[2,16,64,256,4]{2,1,4,0,3:T(8,128)(2,1)}) %all-gather.2.cloned.1.call-update) | async-done | bytes 4194320 | tf_op jit(solution)/shard_map/all_gather | solution.py:85
  563.0 6.5 %fusion.66 = (bf16[1,16,64,256,4]{2,1,4,0,3:T(8,128)(2,1)}, bf16[1,16,64,256,4]{2,1,4,0,3:T(8,128)(2,1)}) fusion(bf16[2,16,64,256,4]{2,1,4,0,3:T(8,128)(2,1)} %all-gather.2.cloned.1.call-done), kind=kLoop, calls=%fused_computation.54 | loop fusion | bytes 8388608 | tf_op jit(solution)/shard_map/slice | solution.py:20
  569.4 5.9 copy.33
  575.3 5.0 copy.34
  580.3 2.2 fusion.26
  582.5 2.2 fusion.29
  584.7 0.6 fusion.47
  585.3 0.6 fusion.41
  585.9 1.1 maximum_multiply_fusion
  (8 shorter events, 0.1 us)
Async XLA Ops:
  6.5 556.4 %all-gather.2.cloned.1.call-start = ((), (), s32[]{:S(2)}) async-start(), calls=%async_computation.1 | async-start | bytes 9437184 | tf_op jit(solution)/shard_map/all_gather | solution.py:85
  8.0 53.9 %collective-permute-start.1 = (bf16[32,4,2048]{2,1,0:T(4,128)(2,1)S(1)}, bf16[32,4,2048]{2,1,0:T(4,128)(2,1)}, u32[]{:S(2)}, u32[]{:S(2)}) collective-permute-start(bf16[32,4,2048]{2,1,0:T(4,128)(2,1)S(1)} %reshape.41), channel_id=1, source_target_pairs={{0,3},{1,4},{2,5},{3,6},{4,7},{5,8},{6,9},{7,10},{8,11},{9,12},{10... | collective-permute-start | bytes 1572872 | tf_op jit(solution)/shard_map/ppermute | solution.py:12
  12.5 49.4 %collective-permute-start.2 = (bf16[32,4,2048]{2,1,0:T(4,128)(2,1)S(1)}, bf16[32,4,2048]{2,1,0:T(4,128)(2,1)}, u32[]{:S(2)}, u32[]{:S(2)}) collective-permute-start(bf16[32,4,2048]{2,1,0:T(4,128)(2,1)S(1)} %reshape.41), channel_id=1, source_target_pairs={{0,2},{1,3},{2,4},{3,5},{4,6},{5,7},{6,8},{7,9},{8,10},{9,11},{10,... | collective-permute-start | bytes 1572872 | tf_op jit(solution)/shard_map/ppermute | solution.py:12
  16.3 45.6 %collective-permute-start.3 = (bf16[32,4,2048]{2,1,0:T(4,128)(2,1)S(1)}, bf16[32,4,2048]{2,1,0:T(4,128)(2,1)}, u32[]{:S(2)}, u32[]{:S(2)}) collective-permute-start(bf16[32,4,2048]{2,1,0:T(4,128)(2,1)S(1)} %reshape.41), channel_id=1, source_target_pairs={{0,1},{1,2},{2,3},{3,4},{4,5},{5,6},{6,7},{7,8},{8,9},{9,10},{10,1... | collective-permute-start | bytes 1572872 | tf_op jit(solution)/shard_map/ppermute | solution.py:12
  20.3 41.6 %collective-permute-start = (bf16[32,3,2048]{2,1,0:T(4,128)(2,1)S(1)}, bf16[32,3,2048]{2,1,0:T(4,128)(2,1)}, u32[]{:S(2)}, u32[]{:S(2)}) collective-permute-start(bf16[32,3,2048]{2,1,0:T(4,128)(2,1)S(1)} %slice.150), channel_id=1, source_target_pairs={{0,4},{1,5},{2,6},{3,7},{4,8},{5,9},{6,10},{7,11},{8,12},{9,13},{1... | collective-permute-start | bytes 1179656 | tf_op jit(solution)/shard_map/ppermute | solution.py:12
Sparse Core Ops, SparseCore 0:
  259.7 303.2 all-gather.1
where the time goes:
time: 605 us; the launch traced here: 594 us
  waiting for transfers between devices  335 us (55%)
  matrix products  143 us (24%)
  blocking collectives  48 us (8%)
  local copies, waits for them, and re-layouts  28.1 us (5%)
  starting transfers between devices  15.5 us (3%)
  between operations  14 us (2%)
  other arithmetic  9.84 us (2%)
    all_gather x1, waiting for transfers between devices, body(): lax.all_gather(spectra_blocks, 'feed', axis=3, tiled=True)  302 us
    dot_general x1, matrix products, body(): jnp.einsum('rn,nk->kr', frame_rows, table_low, preferred_element_type=jnp...  69.2 us
    dot_general x1, matrix products, body(): jnp.einsum('rn,nk->kr', frame_rows, table_high, preferred_element_type=jn...  68.5 us
    all_to_all x1, blocking collectives, body(): lax.all_to_all(spectra_pair, 'tm', split_axis=1, concat_axis=2, tiled=True)  48 us
    ppermute x4, waiting for transfers between devices, shifted(): return lax.ppermute(block, axis, route)  33.1 us
    ppermute x4, starting transfers between devices, shifted(): return lax.ppermute(block, axis, route)  15.5 us
  transfers between devices with their start and end apart: 5, of which 2 were waited for; matrix products, arithmetic and copies ran while one was open for 1% of the time, Pallas kernels for 0%

commit v1 on v0

v1 whole, which is shorter than its diff:
```python
import functools
import math

import jax
import jax.numpy as jnp
import ml_dtypes
import numpy as np
from jax import lax
from jax.experimental import pallas as pl
from jax.experimental.pallas import tpu as pltpu
from jax.sharding import PartitionSpec as P

FRAME = 2048
HALF = FRAME // 2
TAPS = 16
REACH = TAPS - 1
STEPS = 8


def dft_table(feeds, times):
    per_time = HALF // times
    per_device = per_time // feeds
    feed = np.arange(feeds).reshape(feeds, 1, 1)
    time = np.arange(times).reshape(1, times, 1)
    own = np.arange(per_device).reshape(1, 1, per_device)
    channel = (time * per_time + feed * per_device + own).reshape(-1)
    turns = (channel[:, None] * np.arange(FRAME)[None, :]) % FRAME
    angle = turns * (2.0 * math.pi / FRAME)
    table = np.stack([np.cos(angle), -np.sin(angle)], axis=1)
    return table.reshape(2 * HALF, FRAME).astype(ml_dtypes.bfloat16)


def channelize_kernel(first_ref, current, back1, back2, back3, back4, previous, taps, table, out, filtered):
    inputs, block = current.shape
    here = block // FRAME

    @pl.when(pl.program_id(0) == 0)
    def _():
        first = first_ref[0]

        def columns(j, carry):
            lane = pl.multiple_of(j * 128, 128)
            weights = [taps[t : t + 1, pl.ds(lane, 128)] for t in range(TAPS)]
            for row in range(0, inputs, 16):
                rows = pl.ds(row, 16)
                frames = []
                for e in range(REACH):
                    back = (REACH - e + here - 1) // here
                    source = (back1, back2, back3, back4)[back - 1]
                    at = source.shape[1] - (REACH - e - (back - 1) * here) * FRAME
                    moved = source[rows, pl.ds(pl.multiple_of(at + lane, 128), 128)].astype(jnp.float32)
                    held = jnp.minimum(first + e, REACH - 1) * FRAME + lane
                    old = previous[rows, pl.ds(pl.multiple_of(held, 128), 128)].astype(jnp.float32)
                    frames.append(jnp.where(first + e < REACH, old, moved))
                for s in range(here):
                    frames.append(current[rows, pl.ds(pl.multiple_of(s * FRAME + lane, 128), 128)].astype(jnp.float32))
                for s in range(here):
                    total = weights[0] * frames[s]
                    for t in range(1, TAPS):
                        total = total + weights[t] * frames[s + t]
                    filtered[pl.ds(s * inputs + row, 16), pl.ds(lane, 128)] = total.astype(jnp.bfloat16)
            return carry

        lax.fori_loop(0, FRAME // 128, columns, 0)

    spectrum = lax.dot_general(
        table[...], filtered[...], (((1,), (1,)), ((), ())), preferred_element_type=jnp.float32
    )
    out[...] = (spectrum * (1.0 / math.sqrt(FRAME))).astype(jnp.bfloat16)


def channelize(first, current, backs, previous, taps, table):
    inputs, block = current.shape
    rows = inputs * (block // FRAME)
    whole = lambda a: pl.BlockSpec(a.shape, lambda i: (0,) * a.ndim)
    step = table.shape[0] // STEPS
    operands = (current, *backs, previous, taps)
    return pl.pallas_call(
        channelize_kernel,
        grid=(STEPS,),
        out_shape=jax.ShapeDtypeStruct((table.shape[0], rows), jnp.bfloat16),
        in_specs=[pl.BlockSpec(memory_space=pltpu.SMEM)]
        + [whole(a) for a in operands]
        + [pl.BlockSpec((step, FRAME), lambda i: (i, 0))],
        out_specs=pl.BlockSpec((step, rows), lambda i: (i, 0)),
        scratch_shapes=[pltpu.VMEM((rows, FRAME), jnp.bfloat16)],
        compiler_params=pltpu.CompilerParams(vmem_limit_bytes=40 * 2**20),
    )(first, *operands, table)


def correlate_kernel(feeds, inputs, scale, received, out, z_ref, w_ref):
    channels, rows, lanes = received.shape
    wide = rows // feeds
    spectra = lanes // inputs
    sign = jnp.where(lax.broadcasted_iota(jnp.int32, (inputs, wide), 1) < wide // 2, 1.0, -1.0)
    for k in range(channels):
        for f in range(feeds):
            turned = received[k, f * wide : (f + 1) * wide, :].astype(jnp.float32).T
            for s in range(spectra):
                part = turned[s * inputs : (s + 1) * inputs]
                at = (slice(f * inputs, (f + 1) * inputs), slice(s * wide, (s + 1) * wide))
                z_ref[at] = part.astype(jnp.bfloat16)
                w_ref[at] = (pltpu.roll(part, wide // 2, 1) * sign).astype(jnp.bfloat16)
        every = z_ref[...]
        for part, left in enumerate((z_ref, w_ref)):
            sums = lax.dot_general(
                left[...], every, (((1,), (1,)), ((), ())), preferred_element_type=jnp.float32
            )
            sums = (sums * scale).astype(jnp.bfloat16)
            for f in range(feeds):
                out[f, part, k] = sums[f * inputs : (f + 1) * inputs]


def correlate(received, feeds, inputs, scale):
    channels, rows, lanes = received.shape
    total = feeds * inputs
    depth = rows // feeds * (lanes // inputs)
    return pl.pallas_call(
        functools.partial(correlate_kernel, feeds, inputs, scale),
        out_shape=jax.ShapeDtypeStruct((feeds, 2, channels, inputs, total), jnp.bfloat16),
        scratch_shapes=[pltpu.VMEM((total, depth), jnp.bfloat16)] * 2,
        compiler_params=pltpu.CompilerParams(vmem_limit_bytes=32 * 2**20),
    )(received)


def body(table, voltages, previous, filter_taps):
    inputs, block = voltages.shape
    here = block // FRAME
    feeds, times = lax.axis_size("feed"), lax.axis_size("tm")
    count_back = (REACH + here - 1) // here
    backs = []
    for distance in range(1, count_back + 1):
        count = min(here, REACH - (distance - 1) * here)
        route = [(i - distance, i) for i in range(distance, times)]
        backs.append(lax.ppermute(voltages[:, (here - count) * FRAME :], "tm", route))
    first = (lax.axis_index("tm") * here).astype(jnp.int32).reshape(1)
    spectra = channelize(first, voltages, backs, previous, filter_taps, table)
    rows = spectra.shape[1]
    own = HALF // (feeds * times)
    received = lax.all_to_all(
        spectra.reshape(feeds * times, own * 2, rows), ("feed", "tm"), 0, 0, tiled=True
    )
    received = received.reshape(feeds, times, own, 2, rows).transpose(2, 0, 3, 1, 4)
    received = received.reshape(own, feeds * 2 * times, rows)
    result = correlate(received, feeds, inputs, 1.0 / (times * here))
    result = lax.all_to_all(result, "feed", 0, 0, tiled=True)
    result = result.transpose(1, 0, 2, 3, 4).astype(jnp.float32)
    return result.reshape(2, feeds * own, inputs, feeds * inputs)


def solution(mesh):
    sizes = dict(mesh.shape)
    table = dft_table(sizes["feed"], sizes["tm"])
    placed = (P("feed", "tm"), P("feed", None), P())

    def run(voltages, previous, filter_taps):
        return jax.shard_map(
            functools.partial(body, jnp.asarray(table)),
            mesh=mesh,
            in_specs=placed,
            out_specs=P(None, "tm", "feed", None),
            check_vma=False,
        )(voltages, previous, filter_taps)

    return run
```

time: 605 us -> 173 us (0.29)
  the two profiles are of different devices: /device:TPU:98 before, /device:TPU:32 now
where the time goes in v1:
time: 173 us
  blocking collectives  109 us (63%)
  waiting for transfers between devices  30.2 us (17%)
  starting transfers between devices  17.2 us (10%)
  local copies, waits for them, and re-layouts  9.08 us (5%)
  Pallas kernels  6.52 us (4%)
    all_to_all x1, blocking collectives, body(): lax.all_to_all(spectra.reshape(feeds * times, own * 2, rows), ('feed', 't...  71.4 us
    all_to_all x1, blocking collectives, body(): result = lax.all_to_all(result, 'feed', 0, 0, tiled=True)  38 us
    ppermute x4, waiting for transfers between devices, body(): lax.ppermute(voltages[:, (here - count) * FRAME:], 'tm', route)  30.2 us
    ppermute x4, starting transfers between devices, body(): lax.ppermute(voltages[:, (here - count) * FRAME:], 'tm', route)  17.2 us
    unnamed x8, local copies, waits for them, and re-layouts  6.87 us
    pallas_call x1, Pallas kernels, channelize(): pl.pallas_call(channelize_kernel, grid=(STEPS,), out_shape=jax.ShapeDtype...  5.75 us
  transfers between devices with their start and end apart: 4, of which 1 were waited for; matrix products, arithmetic and copies ran while one was open for 1% of the time, Pallas kernels for 0%

profile of v1, /device:TPU:32, one launch (start us, length us, event | category | flops | bytes accessed | tf_op | source)
XLA Modules:
  0.0 172.6 jit_solution(3466468370064867030)
XLA Ops:
  0.0 3.3 %collective-permute-start.2 = (bf16[32,8192]{1,0:T(8,128)(2,1)}, bf16[32,8192]{1,0:T(8,128)(2,1)S(1)}, u32[]{:S(2)}, u32[]{:S(2)}) collective-permute-start(bf16[32,8192]{1,0:T(8,128)(2,1)} %current.1), channel_id=1, source_target_pairs={{0,3},{1,4},{2,5},{3,6},{4,7},{5,8},{6,9},{7,10},{8,11},{9,12},{10... | collective-permute-start | bytes 1572872 | tf_op jit(solution)/shard_map/ppermute | solution.py:135
  3.3 3.8 %collective-permute-start.1 = (bf16[32,8192]{1,0:T(8,128)(2,1)}, bf16[32,8192]{1,0:T(8,128)(2,1)S(1)}, u32[]{:S(2)}, u32[]{:S(2)}) collective-permute-start(bf16[32,8192]{1,0:T(8,128)(2,1)} %current.1), channel_id=1, source_target_pairs={{0,2},{1,3},{2,4},{3,5},{4,6},{5,7},{6,8},{7,9},{8,10},{9,11},{10,... | collective-permute-start | bytes 1572872 | tf_op jit(solution)/shard_map/ppermute | solution.py:135
  7.1 4.9 %collective-permute-start = (bf16[32,8192]{1,0:T(8,128)(2,1)}, bf16[32,8192]{1,0:T(8,128)(2,1)S(1)}, u32[]{:S(2)}, u32[]{:S(2)}) collective-permute-start(bf16[32,8192]{1,0:T(8,128)(2,1)} %current.1), channel_id=1, source_target_pairs={{0,1},{1,2},{2,3},{3,4},{4,5},{5,6},{6,7},{7,8},{8,9},{9,10},{10,1... | collective-permute-start | bytes 1572872 | tf_op jit(solution)/shard_map/ppermute | solution.py:135
  12.0 1.0 slice.3
  13.0 5.2 %collective-permute-start.3 = (bf16[32,6144]{1,0:T(8,128)(2,1)S(1)}, bf16[32,6144]{1,0:T(8,128)(2,1)S(1)}, u32[]{:S(2)}, u32[]{:S(2)}) collective-permute-start(bf16[32,6144]{1,0:T(8,128)(2,1)S(1)} %slice.3), channel_id=1, source_target_pairs={{0,4},{1,5},{2,6},{3,7},{4,8},{5,9},{6,10},{7,11},{8,12},{9,13},{1... | collective-permute-start | bytes 1179656 | tf_op jit(solution)/shard_map/ppermute | solution.py:135
  18.2 30.2 %collective-permute-done.3.back4 = bf16[32,6144]{1,0:T(8,128)(2,1)S(1)} collective-permute-done((bf16[32,6144]{1,0:T(8,128)(2,1)S(1)}, bf16[32,6144]{1,0:T(8,128)(2,1)S(1)}, u32[]{:S(2)}, u32[]{:S(2)}) %collective-permute-start.3) | collective-permute-done | bytes 393248 | tf_op jit(solution)/shard_map/ppermute | solution.py:135
  48.4 0.0 collective-permute-done.2.back3
  48.4 0.0 collective-permute-done.1.back2
  48.5 0.0 collective-permute-done.back1
  48.5 0.0 copy-start
  48.5 3.4 %copy-done = bf16[2048,2048]{1,0:T(8,128)(2,1)S(1)} copy-done((bf16[2048,2048]{1,0:T(8,128)(2,1)S(1)}, bf16[2048,2048]{1,0:T(8,128)(2,1)}, u32[]{:S(2)}) %copy-start) | copy-done | bytes 8388632
  51.8 0.0 copy-start.1
  51.8 1.5 copy-done.1
  53.4 0.0 copy-start.2
  53.4 1.0 copy-done.2
  54.4 0.0 copy-start.3
  54.4 0.9 copy-done.3
  55.3 5.8 %shard_map.46 = bf16[2048,128]{1,0:T(8,128)(2,1)S(1)} custom-call(s32[1]{0:T(128)} %bitcast.first_ref, bf16[32,8192]{1,0:T(8,128)(2,1)S(1)} %copy-done.2, bf16[32,8192]{1,0:T(8,128)(2,1)S(1)} %collective-permute-done.back1, bf16[32,8192]{1,0:T(8,128)(2,1)S(1)} %collective-permute-done.1.back2, bf16[32,8192]{1,0:T(8,128)(2,1)S(1)} %collective-permute-done.2.back3, ...), custom_call_target="tpu_custom_call" | custom-call | tf_op jit(solution)/shard_map/pallas_call | solution.py:78
  61.1 71.4 %all_to_all.10 = bf16[512,4,128]{2,1,0:T(4,128)(2,1)S(1)} all-to-all(bf16[512,4,128]{2,1,0:T(4,128)(2,1)S(1)} %bitcast.10), channel_id=1, replica_groups=mesh['feed'=8,'tm'=64] {'feed','tm'}, dimensions={0} | all-to-all | bytes 1048576 | tf_op jit(solution)/shard_map/all_to_all | solution.py:140
  132.5 0.1 copy.8
  132.6 0.8 shard_map.47
  133.4 38.0 %all_to_all.11 = bf16[8,2,2,32,256]{4,3,2,1,0:T(8,128)(2,1)S(1)} all-to-all(bf16[8,2,2,32,256]{4,3,2,1,0:T(8,128)(2,1)S(1)} %shard_map.47), channel_id=1, replica_groups=mesh['feed'=8,'tm'=64] {'feed'}, dimensions={0} | all-to-all | bytes 1048576 | tf_op jit(solution)/shard_map/all_to_all | solution.py:146
  171.4 0.1 convert_bitcast_fusion
  171.5 1.1 copy.10
  (1 shorter events, 0.0 us)
Async XLA Ops:
  0.0 48.4 %collective-permute-start.2 = (bf16[32,8192]{1,0:T(8,128)(2,1)}, bf16[32,8192]{1,0:T(8,128)(2,1)S(1)}, u32[]{:S(2)}, u32[]{:S(2)}) collective-permute-start(bf16[32,8192]{1,0:T(8,128)(2,1)} %current.1), channel_id=1, source_target_pairs={{0,3},{1,4},{2,5},{3,6},{4,7},{5,8},{6,9},{7,10},{8,11},{9,12},{10... | collective-permute-start | bytes 1572872 | tf_op jit(solution)/shard_map/ppermute | solution.py:135
  3.3 45.2 %collective-permute-start.1 = (bf16[32,8192]{1,0:T(8,128)(2,1)}, bf16[32,8192]{1,0:T(8,128)(2,1)S(1)}, u32[]{:S(2)}, u32[]{:S(2)}) collective-permute-start(bf16[32,8192]{1,0:T(8,128)(2,1)} %current.1), channel_id=1, source_target_pairs={{0,2},{1,3},{2,4},{3,5},{4,6},{5,7},{6,8},{7,9},{8,10},{9,11},{10,... | collective-permute-start | bytes 1572872 | tf_op jit(solution)/shard_map/ppermute | solution.py:135
  7.1 41.4 %collective-permute-start = (bf16[32,8192]{1,0:T(8,128)(2,1)}, bf16[32,8192]{1,0:T(8,128)(2,1)S(1)}, u32[]{:S(2)}, u32[]{:S(2)}) collective-permute-start(bf16[32,8192]{1,0:T(8,128)(2,1)} %current.1), channel_id=1, source_target_pairs={{0,1},{1,2},{2,3},{3,4},{4,5},{5,6},{6,7},{7,8},{8,9},{9,10},{10,1... | collective-permute-start | bytes 1572872 | tf_op jit(solution)/shard_map/ppermute | solution.py:135
  13.0 35.4 %collective-permute-start.3 = (bf16[32,6144]{1,0:T(8,128)(2,1)S(1)}, bf16[32,6144]{1,0:T(8,128)(2,1)S(1)}, u32[]{:S(2)}, u32[]{:S(2)}) collective-permute-start(bf16[32,6144]{1,0:T(8,128)(2,1)S(1)} %slice.3), channel_id=1, source_target_pairs={{0,4},{1,5},{2,6},{3,7},{4,8},{5,9},{6,10},{7,11},{8,12},{9,13},{1... | collective-permute-start | bytes 1179656 | tf_op jit(solution)/shard_map/ppermute | solution.py:135
  48.5 3.4 %copy-start = (bf16[2048,2048]{1,0:T(8,128)(2,1)S(1)}, bf16[2048,2048]{1,0:T(8,128)(2,1)}, u32[]{:S(2)}) copy-start(bf16[2048,2048]{1,0:T(8,128)(2,1)} %constant.8.clone.table) | copy-start | bytes 25165828
  51.8 1.5 copy-start.1
  53.4 1.0 copy-start.2
  54.4 0.9 copy-start.3

commit v2 on v1

v2 whole, which is shorter than its diff:
```python
import functools
import math

import jax
import jax.numpy as jnp
import ml_dtypes
import numpy as np
from jax import lax
from jax.experimental import pallas as pl
from jax.experimental.pallas import tpu as pltpu
from jax.sharding import PartitionSpec as P

FRAME = 2048
HALF = FRAME // 2
TAPS = 16
REACH = TAPS - 1
STEPS = 8
CORES = 2
VMEM_BYTES = 60 * 2**20


def dft_table(feeds, times):
    per_time = HALF // times
    per_device = per_time // feeds
    feed = np.arange(feeds).reshape(feeds, 1, 1)
    time = np.arange(times).reshape(1, times, 1)
    own = np.arange(per_device).reshape(1, 1, per_device)
    channel = (time * per_time + feed * per_device + own).reshape(-1)
    turns = (channel[:, None] * np.arange(FRAME)[None, :]) % FRAME
    angle = turns * (2.0 * math.pi / FRAME)
    table = np.stack([np.cos(angle), -np.sin(angle)], axis=1)
    return table.reshape(2 * HALF, FRAME).astype(ml_dtypes.bfloat16)


def channelize_kernel(place_ref, left, own, right, previous, taps, table, out, filtered):
    cores, inputs, block = own.shape
    here = block // FRAME
    spectra = cores * here
    back = REACH - spectra

    @pl.when(pl.program_id(0) == 0)
    def _():
        chip = place_ref[0]
        at_start = chip == 0
        at_end = chip == place_ref[1] - 1
        first_input = pl.multiple_of(place_ref[2], inputs)

        def columns(j, carry):
            lane = pl.multiple_of(j * 128, 128)
            weights = [taps[t : t + 1, pl.ds(lane, 128)] for t in range(TAPS)]
            frames = []
            for w in range(spectra + REACH):
                source = (left, own, right)[(w + spectra - back) // spectra]
                frame = (w + spectra - back) % spectra
                at = pl.ds(pl.multiple_of(frame % here * FRAME + lane, 128), 128)
                value = source[frame // here, :, at].astype(jnp.float32)
                if w < REACH:
                    held = w if w >= back else jnp.where(at_start, w + spectra, w)
                    at = pl.ds(pl.multiple_of(held * FRAME + lane, 128), 128)
                    old = previous[pl.ds(first_input, inputs), at].astype(jnp.float32)
                    use_old = at_end if w >= back else jnp.logical_or(at_start, at_end)
                    value = jnp.where(use_old, old, value)
                frames.append(value)
            for s in range(spectra):
                total = weights[0] * frames[s]
                for t in range(1, TAPS):
                    total = total + weights[t] * frames[s + t]
                filtered[pl.ds(s * inputs, inputs), pl.ds(lane, 128)] = total.astype(jnp.bfloat16)
            return carry

        lax.fori_loop(0, FRAME // 128, columns, 0)

    spectrum = lax.dot_general(
        table[...], filtered[...], (((1,), (1,)), ((), ())), preferred_element_type=jnp.float32
    )
    out[...] = (spectrum * (1.0 / math.sqrt(FRAME))).astype(jnp.bfloat16)


def channelize(place, left, own, right, previous, taps, table):
    cores, inputs, block = own.shape
    rows = cores * inputs * (block // FRAME)
    whole = lambda a: pl.BlockSpec(a.shape, lambda i: (0,) * a.ndim)
    step = table.shape[0] // STEPS
    operands = (left, own, right, previous, taps)
    return pl.pallas_call(
        channelize_kernel,
        grid=(STEPS,),
        out_shape=jax.ShapeDtypeStruct((table.shape[0], rows), jnp.bfloat16),
        in_specs=[pl.BlockSpec(memory_space=pltpu.SMEM)]
        + [whole(a) for a in operands]
        + [pl.BlockSpec((step, FRAME), lambda i: (i, 0))],
        out_specs=pl.BlockSpec((step, rows), lambda i: (i, 0)),
        scratch_shapes=[pltpu.VMEM((rows, FRAME), jnp.bfloat16)],
        compiler_params=pltpu.CompilerParams(vmem_limit_bytes=VMEM_BYTES),
    )(place, *operands, table)


def correlate_kernel(feeds, inputs, scale, received, out, z_ref, w_ref):
    channels, rows, lanes = received.shape
    wide = rows // feeds
    quarter = wide // 4
    lane = lax.broadcasted_iota(jnp.int32, (inputs, wide), 1)
    sign = jnp.where(lane < wide // 2, 1.0, -1.0)
    low = lane % (2 * quarter) < quarter
    for k in range(channels):
        for f in range(feeds):
            turned = received[k, f * wide : (f + 1) * wide, :].astype(jnp.float32).T
            for pair in range(lanes // inputs // 2):
                even = turned[2 * pair * inputs : (2 * pair + 1) * inputs]
                odd = turned[(2 * pair + 1) * inputs : (2 * pair + 2) * inputs]
                parts = (
                    jnp.where(low, even, pltpu.roll(odd, quarter, 1)),
                    jnp.where(low, pltpu.roll(even, wide - quarter, 1), odd),
                )
                for core, part in enumerate(parts):
                    row = (2 * f + core) * inputs
                    at = (slice(row, row + inputs), slice(pair * wide, (pair + 1) * wide))
                    z_ref[at] = part.astype(jnp.bfloat16)
                    w_ref[at] = (pltpu.roll(part, wide // 2, 1) * sign).astype(jnp.bfloat16)
        every = z_ref[...]
        for part, left in enumerate((z_ref, w_ref)):
            sums = lax.dot_general(
                left[...], every, (((1,), (1,)), ((), ())), preferred_element_type=jnp.float32
            )
            sums = (sums * scale).astype(jnp.bfloat16)
            for f in range(feeds):
                out[f, part, k] = sums[2 * f * inputs : 2 * (f + 1) * inputs]


def correlate(received, feeds, inputs, scale):
    channels, rows, lanes = received.shape
    total = feeds * 2 * inputs
    depth = rows * lanes // total
    return pl.pallas_call(
        functools.partial(correlate_kernel, feeds, inputs, scale),
        out_shape=jax.ShapeDtypeStruct((feeds, 2, channels, 2 * inputs, total), jnp.bfloat16),
        scratch_shapes=[pltpu.VMEM((total, depth), jnp.bfloat16)] * 2,
        compiler_params=pltpu.CompilerParams(vmem_limit_bytes=32 * 2**20),
    )(received)


def body(table, voltages, previous, filter_taps):
    inputs, block = voltages.shape
    feeds, times = lax.axis_size("feed"), lax.axis_size("tm")
    chips = times // CORES
    here = inputs // CORES
    place = lax.axis_index("tm").astype(jnp.int32)
    chip, core = place // CORES, place % CORES
    own = lax.all_to_all(
        voltages.reshape(CORES, here, block), "tm", 0, 0,
        axis_index_groups=[[c * CORES + o for o in range(CORES)] for c in range(chips)], tiled=True,
    )
    ups = [(t, t + CORES) for t in range(times - CORES)]
    downs = [(t, (t - CORES) % times) for t in range(times)]
    right = lax.ppermute(own, "tm", downs)
    left = lax.ppermute(own, "tm", ups)
    numbers = jnp.stack([chip, jnp.int32(chips), core * here])
    spectra = channelize(numbers, left, own, right, previous, filter_taps, table)
    rows = spectra.shape[1]
    per_device = HALF // (feeds * times)
    received = lax.all_to_all(
        spectra.reshape(feeds * times, per_device * 2, rows), ("feed", "tm"), 0, 0, tiled=True
    )
    received = received.reshape(feeds, chips, CORES, per_device, 2, rows).transpose(3, 0, 4, 2, 1, 5)
    received = received.reshape(per_device, feeds * 2 * times, rows)
    result = correlate(received, feeds, here, FRAME / (times * block))
    result = lax.all_to_all(result, "feed", 0, 0, tiled=True)
    result = result.transpose(1, 0, 2, 3, 4).astype(jnp.float32)
    return result.reshape(2, feeds * per_device, inputs, feeds * inputs)


def solution(mesh):
    sizes = dict(mesh.shape)
    table = dft_table(sizes["feed"], sizes["tm"])
    placed = (P("feed", "tm"), P("feed", None), P())

    def run(voltages, previous, filter_taps):
        return jax.shard_map(
            functools.partial(body, jnp.asarray(table)),
            mesh=mesh,
            in_specs=placed,
            out_specs=P(None, "tm", "feed", None),
            check_vma=False,
        )(voltages, previous, filter_taps)

    return run
```

time: 173 us -> 147 us (0.85)
  blocking collectives: 109 us -> 92.6 us
  starting transfers between devices: 17.2 us -> 9.3 us
  local copies, waits for them, and re-layouts: 9.08 us -> 2.06 us
  Pallas kernels: 6.52 us -> 13.5 us
    all_to_all x1 -> x2, blocking collectives: 71.4 us -> 54.8 us  [the longest x1 49.6 us: body(): lax.all_to_all(spectra.reshape(feeds * times, per_device * 2, rows), ('fe...]
    ppermute x4 -> x2, starting transfers between devices: 17.2 us -> 9.3 us  [the longest x1 7.38 us: body(): right = lax.ppermute(own, 'tm', downs)]
    unnamed x8 -> x6, local copies, waits for them, and re-layouts: 6.87 us -> 0.8 us
    pallas_call x1, Pallas kernels: 5.75 us -> 11.1 us  [channelize(): pl.pallas_call(channelize_kernel, grid=(STEPS,), out_shape=jax.ShapeDtype...]
    ppermute x4 -> x2, waiting for transfers between devices: 30.2 us -> 28.7 us  [the longest x1 19.8 us: body(): left = lax.ppermute(own, 'tm', ups)]
  transfers between devices with their start and end apart: 4 -> 2, of which waited for: 1 -> 2; matrix products, arithmetic and copies ran while one was open for 1% -> 0% of each run, Pallas kernels for 0% -> 0%
where the time goes in v2:
time: 147 us
  blocking collectives  92.6 us (63%)
  waiting for transfers between devices  28.7 us (20%)
  Pallas kernels  13.5 us (9%)
  starting transfers between devices  9.3 us (6%)
  local copies, waits for them, and re-layouts  2.06 us (1%)
    all_to_all x1, blocking collectives, body(): lax.all_to_all(spectra.reshape(feeds * times, per_device * 2, rows), ('fe...  49.6 us
    all_to_all x1, blocking collectives, body(): result = lax.all_to_all(result, 'feed', 0, 0, tiled=True)  37.8 us
    ppermute x1, waiting for transfers between devices, body(): left = lax.ppermute(own, 'tm', ups)  19.8 us
    pallas_call x1, Pallas kernels, channelize(): pl.pallas_call(channelize_kernel, grid=(STEPS,), out_shape=jax.ShapeDtype...  11.1 us
    ppermute x1, waiting for transfers between devices, body(): right = lax.ppermute(own, 'tm', downs)  8.84 us
    ppermute x1, starting transfers between devices, body(): right = lax.ppermute(own, 'tm', downs)  7.38 us
    all_to_all x1, blocking collectives, body(): lax.all_to_all(voltages.reshape(CORES, here, block), 'tm', 0, 0, axis_ind...  5.21 us
  transfers between devices with their start and end apart: 2, of which 2 were waited for; matrix products, arithmetic and copies ran while one was open for 0% of the time, Pallas kernels for 0%

profile of v2, /device:TPU:32, one launch (start us, length us, event | category | flops | bytes accessed | tf_op | source)
XLA Modules:
  0.0 146.9 jit_solution(9147090198542545719)
XLA Ops:
  0.0 5.2 %all_to_all.15.own = bf16[2,16,8192]{2,1,0:T(8,128)(2,1)S(1)} all-to-all(bf16[2,16,8192]{2,1,0:T(8,128)(2,1)} %bitcast.14), channel_id=1, replica_groups={{0,1},{2,3},{4,5},{6,7},{8,9},{10,11},{12,13},{14,15},{16,17},{18,19},{..., dimensions={0} | all-to-all | bytes 1048576 | tf_op jit(solution)/shard_map/all_to_all | solution.py:149
  5.2 0.0 copy-start
  5.2 7.4 %collective-permute-start.1 = (bf16[2,16,8192]{2,1,0:T(8,128)(2,1)S(1)}, bf16[2,16,8192]{2,1,0:T(8,128)(2,1)S(1)}, u32[]{:S(2)}, u32[]{:S(2)}) collective-permute-start(bf16[2,16,8192]{2,1,0:T(8,128)(2,1)S(1)} %all_to_all.15.own), channel_id=1, source_target_pairs={{0,62},{1,63},{2,0},{3,1},{4,2},{5,3},{6,4},{7,5},{8,6},{9,7},{10,... | collective-permute-start | bytes 1572872 | tf_op jit(solution)/shard_map/ppermute | solution.py:155
  12.6 1.9 %collective-permute-start = (bf16[2,16,8192]{2,1,0:T(8,128)(2,1)S(1)}, bf16[2,16,8192]{2,1,0:T(8,128)(2,1)S(1)}, u32[]{:S(2)}, u32[]{:S(2)}) collective-permute-start(bf16[2,16,8192]{2,1,0:T(8,128)(2,1)S(1)} %all_to_all.15.own), channel_id=1, source_target_pairs={{0,2},{1,3},{2,4},{3,5},{4,6},{5,7},{6,8},{7,9},{8,10},{9,11},{10,... | collective-permute-start | bytes 1572872 | tf_op jit(solution)/shard_map/ppermute | solution.py:156
  14.6 0.7 pad_add_fusion.place_ref
  15.2 8.8 %collective-permute-done.1.right = bf16[2,16,8192]{2,1,0:T(8,128)(2,1)S(1)} collective-permute-done((bf16[2,16,8192]{2,1,0:T(8,128)(2,1)S(1)}, bf16[2,16,8192]{2,1,0:T(8,128)(2,1)S(1)}, u32[]{:S(2)}, u32[]{:S(2)}) %collective-permute-start.1) | collective-permute-done | bytes 524320 | tf_op jit(solution)/shard_map/ppermute | solution.py:155
  24.1 0.0 copy-start.1
  24.1 19.8 %collective-permute-done.left = bf16[2,16,8192]{2,1,0:T(8,128)(2,1)S(1)} collective-permute-done((bf16[2,16,8192]{2,1,0:T(8,128)(2,1)S(1)}, bf16[2,16,8192]{2,1,0:T(8,128)(2,1)S(1)}, u32[]{:S(2)}, u32[]{:S(2)}) %collective-permute-start) | collective-permute-done | bytes 524320 | tf_op jit(solution)/shard_map/ppermute | solution.py:156
  43.9 0.0 copy-done
  43.9 0.0 copy-done.1
  43.9 0.0 copy-start.2
  43.9 0.8 copy-done.2
  44.7 11.1 %shard_map.46 = bf16[2048,128]{1,0:T(8,128)(2,1)} custom-call(s32[3]{0:T(128)} %pad_add_fusion.place_ref, bf16[2,16,8192]{2,1,0:T(8,128)(2,1)} %copy-done.2, bf16[2,16,8192]{2,1,0:T(8,128)(2,1)} %copy-done, bf16[2,16,8192]{2,1,0:T(8,128)(2,1)} %copy-done.1, bf16[32,30720]{1,0:T(8,128)(2,1)} %previous.1, f32[16,2048]{1,0:T(8,128)} %taps.1, ...), custom_call_target="tpu_custom_call" | custom-call | tf_op jit(solution)/shard_map/pallas_call | solution.py:85
  55.8 49.6 %all_to_all.16 = bf16[512,4,128]{2,1,0:T(4,128)(2,1)S(1)} all-to-all(bf16[512,4,128]{2,1,0:T(4,128)(2,1)} %bitcast.12), channel_id=1, replica_groups=mesh['feed'=8,'tm'=64] {'feed','tm'}, dimensions={0} | all-to-all | bytes 1048576 | tf_op jit(solution)/shard_map/all_to_all | solution.py:161
  105.4 0.1 copy.8
  105.4 0.1 copy.9
  105.6 2.4 %shard_map.47 = bf16[8,2,2,32,256]{4,3,2,1,0:T(8,128)(2,1)S(1)} custom-call(bf16[2,1024,128]{2,1,0:T(8,128)(2,1)S(1)} %bitcast.11), custom_call_target="tpu_custom_call" | custom-call | tf_op jit(solution)/shard_map/pallas_call | solution.py:134
  107.9 37.8 %all_to_all.17 = bf16[8,2,2,32,256]{4,3,2,1,0:T(8,128)(2,1)S(1)} all-to-all(bf16[8,2,2,32,256]{4,3,2,1,0:T(8,128)(2,1)S(1)} %shard_map.47), channel_id=1, replica_groups=mesh['feed'=8,'tm'=64] {'feed'}, dimensions={0} | all-to-all | bytes 1048576 | tf_op jit(solution)/shard_map/all_to_all | solution.py:167
  145.7 0.1 convert_bitcast_fusion
  145.8 1.1 copy.10
Async XLA Ops:
  5.2 38.7 %copy-start = (bf16[2,16,8192]{2,1,0:T(8,128)(2,1)}, bf16[2,16,8192]{2,1,0:T(8,128)(2,1)S(1)}, u32[]{:S(2)}) copy-start(bf16[2,16,8192]{2,1,0:T(8,128)(2,1)S(1)} %all_to_all.15.own) | copy-start | bytes 1572868
  5.2 18.8 %collective-permute-start.1 = (bf16[2,16,8192]{2,1,0:T(8,128)(2,1)S(1)}, bf16[2,16,8192]{2,1,0:T(8,128)(2,1)S(1)}, u32[]{:S(2)}, u32[]{:S(2)}) collective-permute-start(bf16[2,16,8192]{2,1,0:T(8,128)(2,1)S(1)} %all_to_all.15.own), channel_id=1, source_target_pairs={{0,62},{1,63},{2,0},{3,1},{4,2},{5,3},{6,4},{7,5},{8,6},{9,7},{10,... | collective-permute-start | bytes 1572872 | tf_op jit(solution)/shard_map/ppermute | solution.py:155
  12.6 31.3 %collective-permute-start = (bf16[2,16,8192]{2,1,0:T(8,128)(2,1)S(1)}, bf16[2,16,8192]{2,1,0:T(8,128)(2,1)S(1)}, u32[]{:S(2)}, u32[]{:S(2)}) collective-permute-start(bf16[2,16,8192]{2,1,0:T(8,128)(2,1)S(1)} %all_to_all.15.own), channel_id=1, source_target_pairs={{0,2},{1,3},{2,4},{3,5},{4,6},{5,7},{6,8},{7,9},{8,10},{9,11},{10,... | collective-permute-start | bytes 1572872 | tf_op jit(solution)/shard_map/ppermute | solution.py:156
  24.1 19.8 %copy-start.1 = (bf16[2,16,8192]{2,1,0:T(8,128)(2,1)}, bf16[2,16,8192]{2,1,0:T(8,128)(2,1)S(1)}, u32[]{:S(2)}) copy-start(bf16[2,16,8192]{2,1,0:T(8,128)(2,1)S(1)} %collective-permute-done.1.right) | copy-start | bytes 1572868
  43.9 0.8 copy-start.2

commit v3 on v2

v3 whole, which is shorter than its diff:
```python
import functools
import math

import jax
import jax.numpy as jnp
import ml_dtypes
import numpy as np
from jax import lax
from jax.experimental import pallas as pl
from jax.experimental.pallas import tpu as pltpu
from jax.sharding import Mesh
from jax.sharding import PartitionSpec as P

FRAME = 2048
HALF = FRAME // 2
TAPS = 16
REACH = TAPS - 1
STEPS = 2
CORES = 2
VMEM_BYTES = 20 * 2**20
LOAD_BYTES = 12 * 2**20


AXES = {"y": 4, "half": 2, "x": 4, "z": 8, "core": 2}
FEED = ("y", "half")
TIME = ("x", "z", "core")
CHIP = ("x", "z")
ORDER = ("core", "x", "y", "z", "half")
PAIR = 2
BLOCK = AXES["z"] * AXES["half"] * PAIR * 2


def dft_table():
    parity = np.arange(2).reshape(2, 1, 1, 1, 1, 1, 1)
    core = np.arange(2).reshape(1, 2, 1, 1, 1, 1, 1)
    x = np.arange(4).reshape(1, 1, 4, 1, 1, 1, 1)
    upper = np.arange(2).reshape(1, 1, 1, 2, 1, 1, 1)
    z = np.arange(8).reshape(1, 1, 1, 1, 8, 1, 1)
    half = np.arange(2).reshape(1, 1, 1, 1, 1, 2, 1)
    pair = np.arange(PAIR).reshape(1, 1, 1, 1, 1, 1, PAIR)
    time = (x * 8 + z) * 2 + core
    channel = time * 16 + pair * 8 + upper * 4 + half * 2 + parity
    turns = (channel.reshape(-1, 1) * np.arange(FRAME // 2)[None, :]) % FRAME
    angle = turns * (2.0 * math.pi / FRAME)
    table = np.stack([np.cos(angle), -np.sin(angle)], axis=1)
    return table.reshape(2, HALF, FRAME // 2).astype(ml_dtypes.bfloat16)


def load_kernel(first_ref, table, previous, table_here, previous_here, arrived):
    inputs = previous_here.shape[0]
    rows = pl.ds(pl.multiple_of(first_ref[0], inputs), inputs)
    copies = (
        pltpu.make_async_copy(table, table_here, arrived.at[0]),
        pltpu.make_async_copy(previous.at[rows], previous_here, arrived.at[1]),
    )
    for copy in copies:
        copy.start()
    for copy in copies:
        copy.wait()


def load(first, table, previous, inputs):
    on_chip = pl.BlockSpec(memory_space=pltpu.VMEM)
    return pl.pallas_call(
        load_kernel,
        out_shape=(
            jax.ShapeDtypeStruct(table.shape, table.dtype),
            jax.ShapeDtypeStruct((inputs, previous.shape[1]), previous.dtype),
        ),
        in_specs=[pl.BlockSpec(memory_space=pltpu.SMEM)] + [pl.BlockSpec(memory_space=pl.ANY)] * 2,
        out_specs=(on_chip, on_chip),
        scratch_shapes=[pltpu.SemaphoreType.DMA((2,))],
        compiler_params=pltpu.CompilerParams(vmem_limit_bytes=LOAD_BYTES),
    )(first, table, previous)


def channelize_kernel(place_ref, left, own, right, previous, taps, table, out, folded):
    cores, inputs, block = own.shape
    here = block // FRAME
    spectra = cores * here
    back = REACH - spectra
    chip = place_ref[0]
    at_start = chip == 0
    at_end = chip == place_ref[1] - 1

    def columns(j, carry):
        parts = []
        for part in range(2):
            lane = pl.multiple_of(part * (FRAME // 2) + j * 128, 128)
            weights = [taps[t : t + 1, pl.ds(lane, 128)] for t in range(TAPS)]
            frames = []
            for w in range(spectra + REACH):
                source = (left, own, right)[(w + spectra - back) // spectra]
                frame = (w + spectra - back) % spectra
                at = pl.ds(pl.multiple_of(frame % here * FRAME + lane, 128), 128)
                value = source[frame // here, :, at].astype(jnp.float32)
                if w < REACH:
                    held = w if w >= back else jnp.where(at_start, w + spectra, w)
                    at = pl.ds(pl.multiple_of(held * FRAME + lane, 128), 128)
                    old = previous[:, at].astype(jnp.float32)
                    use_old = at_end if w >= back else jnp.logical_or(at_start, at_end)
                    value = jnp.where(use_old, old, value)
                frames.append(value)
            totals = []
            for s in range(spectra):
                total = weights[0] * frames[s]
                for t in range(1, TAPS):
                    total = total + weights[t] * frames[s + t]
                totals.append(total)
            parts.append(totals)
        at = pl.ds(pl.multiple_of(j * 128, 128), 128)
        for s, (low, high) in enumerate(zip(*parts)):
            rows = pl.ds(s * inputs, inputs)
            folded[0, rows, at] = (low + high).astype(jnp.bfloat16)
            folded[1, rows, at] = (low - high).astype(jnp.bfloat16)
        return carry

    lax.fori_loop(0, FRAME // 2 // 128, columns, 0)
    step = table.shape[1] // STEPS
    for parity in range(2):
        for j in range(STEPS):
            spectrum = lax.dot_general(
                table[parity, j * step : (j + 1) * step, :],
                folded[parity],
                (((1,), (1,)), ((), ())),
                preferred_element_type=jnp.float32,
            )
            spectrum = (spectrum * (1.0 / math.sqrt(FRAME))).astype(jnp.bfloat16)
            for block in range(step // BLOCK):
                row = ((j * (step // BLOCK) + block) * 2 + parity) * BLOCK
                out[row : row + BLOCK, :] = spectrum[block * BLOCK : (block + 1) * BLOCK]


def channelize(place, left, own, right, previous, taps, table):
    cores, inputs, block = own.shape
    rows = cores * inputs * (block // FRAME)
    on_chip = pl.BlockSpec(memory_space=pltpu.VMEM)
    return pl.pallas_call(
        channelize_kernel,
        out_shape=jax.ShapeDtypeStruct((2 * table.shape[1], rows), jnp.bfloat16),
        in_specs=[pl.BlockSpec(memory_space=pltpu.SMEM)] + [on_chip] * 6,
        out_specs=on_chip,
        scratch_shapes=[pltpu.VMEM((2, rows, FRAME // 2), jnp.bfloat16)],
        compiler_params=pltpu.CompilerParams(vmem_limit_bytes=VMEM_BYTES),
    )(place, left, own, right, previous, taps, table)


def correlate_kernel(feeds, inputs, scale, received, out, both):
    channels, rows, lanes = received.shape
    wide = rows // feeds
    quarter = wide // 4
    total = both.shape[1] // 2
    lane = lax.broadcasted_iota(jnp.int32, (inputs, wide), 1)
    sign = jnp.where(lane < wide // 2, 1.0, -1.0)
    low = lane % (2 * quarter) < quarter
    for k in range(channels):
        for f in range(feeds):
            turned = received[k, f * wide : (f + 1) * wide, :].T.astype(jnp.float32)
            for pair in range(lanes // inputs // 2):
                even = turned[2 * pair * inputs : (2 * pair + 1) * inputs]
                odd = turned[(2 * pair + 1) * inputs : (2 * pair + 2) * inputs]
                parts = (
                    jnp.where(low, even, pltpu.roll(odd, quarter, 1)),
                    jnp.where(low, pltpu.roll(even, wide - quarter, 1), odd),
                )
                for core, part in enumerate(parts):
                    row = (2 * f + core) * inputs
                    at = slice(pair * wide, (pair + 1) * wide)
                    both[k, row : row + inputs, at] = part.astype(jnp.bfloat16)
                    part = pltpu.roll(part, wide // 2, 1) * sign
                    both[k, total + row : total + row + inputs, at] = part.astype(jnp.bfloat16)
    for k in range(channels):
        sums = lax.dot_general(
            both[k], both[k, :total], (((1,), (1,)), ((), ())), preferred_element_type=jnp.float32
        )
        sums = (sums * scale).astype(jnp.bfloat16)
        for part in range(2):
            for f in range(feeds):
                row = part * total + 2 * f * inputs
                out[f, part, k] = sums[row : row + 2 * inputs]


def correlate(received, feeds, inputs, scale):
    channels, rows, lanes = received.shape
    total = feeds * 2 * inputs
    depth = rows * lanes // total
    return pl.pallas_call(
        functools.partial(correlate_kernel, feeds, inputs, scale),
        out_shape=jax.ShapeDtypeStruct((feeds, 2, channels, 2 * inputs, total), jnp.bfloat16),
        scratch_shapes=[pltpu.VMEM((channels, 2 * total, depth), jnp.bfloat16)],
        compiler_params=pltpu.CompilerParams(vmem_limit_bytes=32 * 2**20),
    )(received)


def body(table, voltages, previous, filter_taps):
    inputs, block = voltages.shape
    feeds, chips = math.prod(AXES[a] for a in FEED), math.prod(AXES[a] for a in CHIP)
    here = inputs // CORES
    chip, core = lax.axis_index(CHIP), lax.axis_index("core")
    own = lax.all_to_all(voltages.reshape(CORES, here, block), "core", 0, 0, tiled=True)
    right = lax.ppermute(own, CHIP, [(c, (c - 1) % chips) for c in range(chips)])
    left = lax.ppermute(own, CHIP, [(c, c + 1) for c in range(chips - 1)])
    first = (core * here).astype(jnp.int32).reshape(1)
    table, old = load(first, table, previous, here)
    numbers = jnp.stack([chip.astype(jnp.int32), jnp.int32(chips)])
    spectra = channelize(numbers, left, own, right, old, filter_taps, table)
    rows = spectra.shape[1]
    devices = math.prod(AXES.values())
    received = lax.all_to_all(spectra.reshape(devices, PAIR * 2, rows), ORDER, 0, 0, tiled=True)
    received = received.reshape(*(AXES[a] for a in ORDER), PAIR, 2, rows)
    received = received.transpose(5, 2, 4, 6, 0, 1, 3, 7).reshape(PAIR, -1, rows)
    result = correlate(received, feeds, here, FRAME / (chips * CORES * block))
    result = lax.all_to_all(result, FEED, 0, 0, tiled=True)
    result = result.reshape(2, 2, 2, 2, PAIR, inputs, feeds * inputs).transpose(3, 4, 0, 2, 1, 5, 6)
    return result.astype(jnp.float32).reshape(2, feeds * PAIR, inputs, feeds * inputs)


def solution(mesh):
    parts = Mesh(mesh.devices.reshape(tuple(AXES.values())), tuple(AXES))
    table = dft_table()
    placed = (P(FEED, TIME), P(FEED, None), P())

    def run(voltages, previous, filter_taps):
        return jax.shard_map(
            functools.partial(body, jnp.asarray(table)),
            mesh=parts,
            in_specs=placed,
            out_specs=P(None, TIME, FEED, None),
            check_vma=False,
        )(voltages, previous, filter_taps)

    return run
```

time: 147 us -> 137 us (0.932)
  the two profiles are of different devices: /device:TPU:32 before, /device:TPU:36 now
where the time goes in v3:
time: 137 us
  blocking collectives  93.9 us (69%)
  waiting for transfers between devices  26.2 us (19%)
  starting transfers between devices  5.83 us (4%)
  Pallas kernels  5.56 us (4%)
  local copies, waits for them, and re-layouts  5 us (4%)
    all_to_all x1, blocking collectives, body(): lax.all_to_all(spectra.reshape(devices, PAIR * 2, rows), ORDER, 0, 0, til...  47.8 us
    all_to_all x1, blocking collectives, body(): result = lax.all_to_all(result, FEED, 0, 0, tiled=True)  40.8 us
    ppermute x1, waiting for transfers between devices, body(): left = lax.ppermute(own, CHIP, [(c, c + 1) for c in range(chips - 1)])  20.4 us
    ppermute x1, waiting for transfers between devices, body(): lax.ppermute(own, CHIP, [(c, (c - 1) % chips) for c in range(chips)])  5.75 us
    all_to_all x1, blocking collectives, body(): lax.all_to_all(voltages.reshape(CORES, here, block), 'core', 0, 0, tiled=...  5.35 us
    ppermute x1, starting transfers between devices, body(): left = lax.ppermute(own, CHIP, [(c, c + 1) for c in range(chips - 1)])  3.83 us
    unnamed x6, local copies, waits for them, and re-layouts  3.73 us
    pallas_call x1, Pallas kernels, channelize(): pl.pallas_call(channelize_kernel, out_shape=jax.ShapeDtypeStruct((2 * tab...  3.52 us
  transfers between devices with their start and end apart: 2, of which 2 were waited for; matrix products, arithmetic and copies ran while one was open for 0% of the time, Pallas kernels for 0%

profile of v3, /device:TPU:36, one launch (start us, length us, event | category | flops | bytes accessed | tf_op | source)
XLA Modules:
  0.0 136.7 jit_solution(10311975888002545178)
XLA Ops:
  0.0 0.0 copy-start.2
  0.0 5.3 %all_to_all.15.own = bf16[2,16,8192]{2,1,0:T(8,128)(2,1)S(1)} all-to-all(bf16[2,16,8192]{2,1,0:T(8,128)(2,1)} %bitcast.17), channel_id=1, replica_groups=mesh['y'=4,'half'=2,'x'=4,'z'=8,'core'=2] {'core'}, dimensions={0} | all-to-all | bytes 1048576 | tf_op jit(solution)/shard_map/all_to_all | solution.py:200
  5.3 2.0 %collective-permute-start.1 = (bf16[2,16,8192]{2,1,0:T(8,128)(2,1)S(1)}, bf16[2,16,8192]{2,1,0:T(8,128)(2,1)S(1)}, u32[]{:S(2)}, u32[]{:S(2)}) collective-permute-start(bf16[2,16,8192]{2,1,0:T(8,128)(2,1)S(1)} %all_to_all.15.own), channel_id=1, source_target_pairs={{0,62},{2,0},{4,2},{6,4},{8,6},{10,8},{12,10},{14,12},{16,14},{18,... | collective-permute-start | bytes 1572872 | tf_op jit(solution)/shard_map/ppermute | solution.py:201
  7.4 3.8 %collective-permute-start = (bf16[2,16,8192]{2,1,0:T(8,128)(2,1)S(1)}, bf16[2,16,8192]{2,1,0:T(8,128)(2,1)S(1)}, u32[]{:S(2)}, u32[]{:S(2)}) collective-permute-start(bf16[2,16,8192]{2,1,0:T(8,128)(2,1)S(1)} %all_to_all.15.own), channel_id=1, source_target_pairs={{0,2},{2,4},{4,6},{6,8},{8,10},{10,12},{12,14},{14,16},{16,18},{18... | collective-permute-start | bytes 1572872 | tf_op jit(solution)/shard_map/ppermute | solution.py:202
  11.2 0.0 copy-start
  11.2 2.2 %copy-done = bf16[2,1024,1024]{2,1,0:T(8,128)(2,1)S(1)} copy-done((bf16[2,1024,1024]{2,1,0:T(8,128)(2,1)S(1)}, bf16[2,1024,1024]{2,1,0:T(8,128)(2,1)}, u32[]{:S(2)}) %copy-start) | copy-done | bytes 4194328
  13.4 0.0 copy-start.1
  13.4 1.5 %copy-done.1 = bf16[32,30720]{1,0:T(8,128)(2,1)S(1)} copy-done((bf16[32,30720]{1,0:T(8,128)(2,1)S(1)}, bf16[32,30720]{1,0:T(8,128)(2,1)}, u32[]{:S(2)}) %copy-start.1) | copy-done | bytes 1966104
  14.9 0.6 shard_map.46
  15.6 0.1 pad_add_fusion.place_ref
  15.6 5.8 %collective-permute-done.1.right = bf16[2,16,8192]{2,1,0:T(8,128)(2,1)S(1)} collective-permute-done((bf16[2,16,8192]{2,1,0:T(8,128)(2,1)S(1)}, bf16[2,16,8192]{2,1,0:T(8,128)(2,1)S(1)}, u32[]{:S(2)}, u32[]{:S(2)}) %collective-permute-start.1) | collective-permute-done | bytes 524320 | tf_op jit(solution)/shard_map/ppermute | solution.py:201
  21.4 20.4 %collective-permute-done.left = bf16[2,16,8192]{2,1,0:T(8,128)(2,1)S(1)} collective-permute-done((bf16[2,16,8192]{2,1,0:T(8,128)(2,1)S(1)}, bf16[2,16,8192]{2,1,0:T(8,128)(2,1)S(1)}, u32[]{:S(2)}, u32[]{:S(2)}) %collective-permute-start) | collective-permute-done | bytes 524320 | tf_op jit(solution)/shard_map/ppermute | solution.py:202
  41.8 0.0 copy-done.2
  41.8 3.5 %shard_map.47 = bf16[2048,128]{1,0:T(8,128)(2,1)S(1)} custom-call(s32[2]{0:T(128)S(1)} %pad_add_fusion.place_ref, bf16[2,16,8192]{2,1,0:T(8,128)(2,1)S(1)} %collective-permute-done.left, bf16[2,16,8192]{2,1,0:T(8,128)(2,1)S(1)} %all_to_all.15.own, bf16[2,16,8192]{2,1,0:T(8,128)(2,1)S(1)} %collective-permute-done.1.right, ...), custom_call_target="tpu_custom_call" | custom-call | tf_op jit(solution)/shard_map/pallas_call | solution.py:138
  45.3 47.8 %all_to_all.16 = bf16[512,4,128]{2,1,0:T(4,128)(2,1)S(1)} all-to-all(bf16[512,4,128]{2,1,0:T(4,128)(2,1)S(1)} %bitcast.13), channel_id=1, replica_groups=mesh['y'=4,'half'=2,'x'=4,'z'=8,'core'=2] {'core','x','y','z','half'}, dimensions={0} | all-to-all | bytes 1048576 | tf_op jit(solution)/shard_map/all_to_all | solution.py:209
  93.1 0.1 copy.9
  93.2 0.1 copy.10
  93.3 1.4 %shard_map.48 = bf16[8,2,2,32,256]{4,3,2,1,0:T(8,128)(2,1)S(1)} custom-call(bf16[2,1024,128]{2,1,0:T(8,128)(2,1)S(1)} %bitcast.14), custom_call_target="tpu_custom_call" | custom-call | tf_op jit(solution)/shard_map/pallas_call | solution.py:187
  94.8 40.8 %all_to_all.17 = bf16[8,2,2,32,256]{4,3,2,1,0:T(8,128)(2,1)S(1)} all-to-all(bf16[8,2,2,32,256]{4,3,2,1,0:T(8,128)(2,1)S(1)} %shard_map.48), channel_id=1, replica_groups=mesh['y'=4,'half'=2,'x'=4,'z'=8,'core'=2] {'y','half'}, dimensions={0} | all-to-all | bytes 1048576 | tf_op jit(solution)/shard_map/all_to_all | solution.py:213
  135.5 0.1 convert_bitcast_fusion
  135.7 1.1 copy.11
Async XLA Ops:
  0.0 41.8 %copy-start.2 = (f32[16,2048]{1,0:T(8,128)S(1)}, f32[16,2048]{1,0:T(8,128)}, u32[]{:S(2)}) copy-start(f32[16,2048]{1,0:T(8,128)} %taps.1) | copy-start | bytes 393220
  5.3 16.0 %collective-permute-start.1 = (bf16[2,16,8192]{2,1,0:T(8,128)(2,1)S(1)}, bf16[2,16,8192]{2,1,0:T(8,128)(2,1)S(1)}, u32[]{:S(2)}, u32[]{:S(2)}) collective-permute-start(bf16[2,16,8192]{2,1,0:T(8,128)(2,1)S(1)} %all_to_all.15.own), channel_id=1, source_target_pairs={{0,62},{2,0},{4,2},{6,4},{8,6},{10,8},{12,10},{14,12},{16,14},{18,... | collective-permute-start | bytes 1572872 | tf_op jit(solution)/shard_map/ppermute | solution.py:201
  7.4 34.4 %collective-permute-start = (bf16[2,16,8192]{2,1,0:T(8,128)(2,1)S(1)}, bf16[2,16,8192]{2,1,0:T(8,128)(2,1)S(1)}, u32[]{:S(2)}, u32[]{:S(2)}) collective-permute-start(bf16[2,16,8192]{2,1,0:T(8,128)(2,1)S(1)} %all_to_all.15.own), channel_id=1, source_target_pairs={{0,2},{2,4},{4,6},{6,8},{8,10},{10,12},{12,14},{14,16},{16,18},{18... | collective-permute-start | bytes 1572872 | tf_op jit(solution)/shard_map/ppermute | solution.py:202
  11.2 2.2 %copy-start = (bf16[2,1024,1024]{2,1,0:T(8,128)(2,1)S(1)}, bf16[2,1024,1024]{2,1,0:T(8,128)(2,1)}, u32[]{:S(2)}) copy-start(bf16[2,1024,1024]{2,1,0:T(8,128)(2,1)} %constant.22.clone.table) | copy-start | bytes 12582916
  13.4 1.5 %copy-start.1 = (bf16[32,30720]{1,0:T(8,128)(2,1)S(1)}, bf16[32,30720]{1,0:T(8,128)(2,1)}, u32[]{:S(2)}) copy-start(bf16[32,30720]{1,0:T(8,128)(2,1)} %previous.1) | copy-start | bytes 5898244

commit v4 on v3

--- a/solution.py
+++ b/solution.py
@@ -25,21 +25,19 @@
 FEED = ("y", "half")
 TIME = ("x", "z", "core")
 CHIP = ("x", "z")
-ORDER = ("core", "x", "y", "z", "half")
-PAIR = 2
-BLOCK = AXES["z"] * AXES["half"] * PAIR * 2
+ORDER = ("half", "core", "x", "y", "z")
+CHANNELS = 4
+BLOCK = AXES["z"] * CHANNELS * 2
 
 
 def dft_table():
-    parity = np.arange(2).reshape(2, 1, 1, 1, 1, 1, 1)
-    core = np.arange(2).reshape(1, 2, 1, 1, 1, 1, 1)
-    x = np.arange(4).reshape(1, 1, 4, 1, 1, 1, 1)
-    upper = np.arange(2).reshape(1, 1, 1, 2, 1, 1, 1)
-    z = np.arange(8).reshape(1, 1, 1, 1, 8, 1, 1)
-    half = np.arange(2).reshape(1, 1, 1, 1, 1, 2, 1)
-    pair = np.arange(PAIR).reshape(1, 1, 1, 1, 1, 1, PAIR)
-    time = (x * 8 + z) * 2 + core
-    channel = time * 16 + pair * 8 + upper * 4 + half * 2 + parity
+    parity = np.arange(2).reshape(2, 1, 1, 1, 1, 1)
+    core = np.arange(2).reshape(1, 2, 1, 1, 1, 1)
+    x = np.arange(4).reshape(1, 1, 4, 1, 1, 1)
+    upper = np.arange(2).reshape(1, 1, 1, 2, 1, 1)
+    z = np.arange(8).reshape(1, 1, 1, 1, 8, 1)
+    own = np.arange(CHANNELS).reshape(1, 1, 1, 1, 1, CHANNELS)
+    channel = ((x * 8 + z) * 2 + core) * 16 + own * 4 + upper * 2 + parity
     turns = (channel.reshape(-1, 1) * np.arange(FRAME // 2)[None, :]) % FRAME
     angle = turns * (2.0 * math.pi / FRAME)
     table = np.stack([np.cos(angle), -np.sin(angle)], axis=1)
@@ -128,7 +126,8 @@
             spectrum = (spectrum * (1.0 / math.sqrt(FRAME))).astype(jnp.bfloat16)
             for block in range(step // BLOCK):
                 row = ((j * (step // BLOCK) + block) * 2 + parity) * BLOCK
-                out[row : row + BLOCK, :] = spectrum[block * BLOCK : (block + 1) * BLOCK]
+                for half in range(out.shape[0]):
+                    out[half, row : row + BLOCK, :] = spectrum[block * BLOCK : (block + 1) * BLOCK]
 
 
 def channelize(place, left, own, right, previous, taps, table):
@@ -137,7 +136,7 @@
     on_chip = pl.BlockSpec(memory_space=pltpu.VMEM)
     return pl.pallas_call(
         channelize_kernel,
-        out_shape=jax.ShapeDtypeStruct((2 * table.shape[1], rows), jnp.bfloat16),
+        out_shape=jax.ShapeDtypeStruct((AXES["half"], 2 * table.shape[1], rows), jnp.bfloat16),
         in_specs=[pl.BlockSpec(memory_space=pltpu.SMEM)] + [on_chip] * 6,
         out_specs=on_chip,
         scratch_shapes=[pltpu.VMEM((2, rows, FRAME // 2), jnp.bfloat16)],
@@ -145,51 +144,62 @@
     )(place, left, own, right, previous, taps, table)
 
 
-def correlate_kernel(feeds, inputs, scale, received, out, both):
+def correlate_kernel(inputs, scale, place_ref, received, out, every, own):
     channels, rows, lanes = received.shape
-    wide = rows // feeds
+    halves, count = AXES["half"], AXES["y"]
+    wide = rows // (halves * count)
     quarter = wide // 4
-    total = both.shape[1] // 2
+    block = 2 * inputs
     lane = lax.broadcasted_iota(jnp.int32, (inputs, wide), 1)
-    sign = jnp.where(lane < wide // 2, 1.0, -1.0)
     low = lane % (2 * quarter) < quarter
+    sign = jnp.where(lax.broadcasted_iota(jnp.int32, (block, wide), 1) < wide // 2, 1.0, -1.0)
     for k in range(channels):
-        for f in range(feeds):
-            turned = received[k, f * wide : (f + 1) * wide, :].T.astype(jnp.float32)
+        for half in range(halves):
+            for y in range(count):
+                first = (half * count + y) * wide
+                turned = received[k, first : first + wide, :].T.astype(jnp.float32)
+                for pair in range(lanes // inputs // 2):
+                    even = turned[2 * pair * inputs : (2 * pair + 1) * inputs]
+                    odd = turned[(2 * pair + 1) * inputs : (2 * pair + 2) * inputs]
+                    parts = (
+                        jnp.where(low, even, pltpu.roll(odd, quarter, 1)),
+                        jnp.where(low, pltpu.roll(even, wide - quarter, 1), odd),
+                    )
+                    for core, part in enumerate(parts):
+                        row = (y * halves + half) * block + core * inputs
+                        at = slice(pair * wide, (pair + 1) * wide)
+                        every[k, row : row + inputs, at] = part.astype(jnp.bfloat16)
+        for y in range(count):
+            row = pl.multiple_of((y * halves + place_ref[2]) * block, block)
             for pair in range(lanes // inputs // 2):
-                even = turned[2 * pair * inputs : (2 * pair + 1) * inputs]
-                odd = turned[(2 * pair + 1) * inputs : (2 * pair + 2) * inputs]
-                parts = (
-                    jnp.where(low, even, pltpu.roll(odd, quarter, 1)),
-                    jnp.where(low, pltpu.roll(even, wide - quarter, 1), odd),
-                )
-                for core, part in enumerate(parts):
-                    row = (2 * f + core) * inputs
-                    at = slice(pair * wide, (pair + 1) * wide)
-                    both[k, row : row + inputs, at] = part.astype(jnp.bfloat16)
-                    part = pltpu.roll(part, wide // 2, 1) * sign
-                    both[k, total + row : total + row + inputs, at] = part.astype(jnp.bfloat16)
+                at = slice(pair * wide, (pair + 1) * wide)
+                part = every[k, pl.ds(row, block), at]
+                own[k, y * block : (y + 1) * block, at] = part
+                part = pltpu.roll(part.astype(jnp.float32), wide // 2, 1) * sign
+                own[k, (count + y) * block : (count + y + 1) * block, at] = part.astype(jnp.bfloat16)
     for k in range(channels):
         sums = lax.dot_general(
-            both[k], both[k, :total], (((1,), (1,)), ((), ())), preferred_element_type=jnp.float32
+            own[k], every[k], (((1,), (1,)), ((), ())), preferred_element_type=jnp.float32
         )
         sums = (sums * scale).astype(jnp.bfloat16)
         for part in range(2):
-            for f in range(feeds):
-                row = part * total + 2 * f * inputs
-                out[f, part, k] = sums[row : row + 2 * inputs]
-
-
-def correlate(received, feeds, inputs, scale):
+            for y in range(count):
+                row = (part * count + y) * block
+                out[y, part, k] = sums[row : row + block]
+
+
+def correlate(place, received, inputs, scale):
     channels, rows, lanes = received.shape
-    total = feeds * 2 * inputs
+    count, total = AXES["y"], AXES["y"] * AXES["half"] * 2 * inputs
     depth = rows * lanes // total
     return pl.pallas_call(
-        functools.partial(correlate_kernel, feeds, inputs, scale),
-        out_shape=jax.ShapeDtypeStruct((feeds, 2, channels, 2 * inputs, total), jnp.bfloat16),
-        scratch_shapes=[pltpu.VMEM((channels, 2 * total, depth), jnp.bfloat16)],
+        functools.partial(correlate_kernel, inputs, scale),
+        out_shape=jax.ShapeDtypeStruct((count, 2, channels, 2 * inputs, total), jnp.bfloat16),
+        in_specs=[pl.BlockSpec(memory_space=pltpu.SMEM), pl.BlockSpec(memory_space=pltpu.VMEM)],
+        out_specs=pl.BlockSpec(memory_space=pltpu.VMEM),
+        scratch_shapes=[pltpu.VMEM((channels, total, depth), jnp.bfloat16)] * 2,
         compiler_params=pltpu.CompilerParams(vmem_limit_bytes=32 * 2**20),
-    )(received)
+    )(place, received)
 
 
 def body(table, voltages, previous, filter_taps):
@@ -202,17 +212,17 @@
     left = lax.ppermute(own, CHIP, [(c, c + 1) for c in range(chips - 1)])
     first = (core * here).astype(jnp.int32).reshape(1)
     table, old = load(first, table, previous, here)
-    numbers = jnp.stack([chip.astype(jnp.int32), jnp.int32(chips)])
+    numbers = jnp.stack([chip.astype(jnp.int32), jnp.int32(chips), lax.axis_index("half").astype(jnp.int32)])
     spectra = channelize(numbers, left, own, right, old, filter_taps, table)
-    rows = spectra.shape[1]
+    rows = spectra.shape[2]
     devices = math.prod(AXES.values())
-    received = lax.all_to_all(spectra.reshape(devices, PAIR * 2, rows), ORDER, 0, 0, tiled=True)
-    received = received.reshape(*(AXES[a] for a in ORDER), PAIR, 2, rows)
-    received = received.transpose(5, 2, 4, 6, 0, 1, 3, 7).reshape(PAIR, -1, rows)
-    result = correlate(received, feeds, here, FRAME / (chips * CORES * block))
-    result = lax.all_to_all(result, FEED, 0, 0, tiled=True)
-    result = result.reshape(2, 2, 2, 2, PAIR, inputs, feeds * inputs).transpose(3, 4, 0, 2, 1, 5, 6)
-    return result.astype(jnp.float32).reshape(2, feeds * PAIR, inputs, feeds * inputs)
+    received = lax.all_to_all(spectra.reshape(devices, CHANNELS * 2, rows), ORDER, 0, 0, tiled=True)
+    received = received.reshape(*(AXES[a] for a in ORDER), CHANNELS, 2, rows)
+    received = received.transpose(5, 0, 3, 6, 1, 2, 4, 7).reshape(CHANNELS, -1, rows)
+    result = correlate(numbers, received, here, FRAME / (chips * CORES * block))
+    result = lax.all_to_all(result, "y", 0, 0, tiled=True)
+    result = result.transpose(1, 2, 0, 3, 4).astype(jnp.float32)
+    return result.reshape(2, AXES["y"] * CHANNELS, inputs, feeds * inputs)
 
 
 def solution(mesh):

time: 137 us -> 136 us (level)
  the two profiles are of different devices: /device:TPU:36 before, /device:TPU:1 now
where the time goes in v4:
time: 136 us; the launch traced here: 135 us
  blocking collectives  96.3 us (71%)
  waiting for transfers between devices  16.4 us (12%)
  starting transfers between devices  11 us (8%)
  Pallas kernels  6.15 us (5%)
  local copies, waits for them, and re-layouts  5.24 us (4%)
    all_to_all x1, blocking collectives, body(): lax.all_to_all(spectra.reshape(devices, CHANNELS * 2, rows), ORDER, 0, 0,...  72.5 us
    all_to_all x1, blocking collectives, body(): result = lax.all_to_all(result, 'y', 0, 0, tiled=True)  12 us
    all_to_all x1, blocking collectives, body(): lax.all_to_all(voltages.reshape(CORES, here, block), 'core', 0, 0, tiled=...  11.9 us
    ppermute x1, waiting for transfers between devices, body(): left = lax.ppermute(own, CHIP, [(c, c + 1) for c in range(chips - 1)])  11.2 us
    ppermute x1, starting transfers between devices, body(): lax.ppermute(own, CHIP, [(c, (c - 1) % chips) for c in range(chips)])  9.69 us
    ppermute x1, waiting for transfers between devices, body(): lax.ppermute(own, CHIP, [(c, (c - 1) % chips) for c in range(chips)])  5.2 us
    unnamed x6, local copies, waits for them, and re-layouts  3.73 us
    pallas_call x1, Pallas kernels, channelize(): pl.pallas_call(channelize_kernel, out_shape=jax.ShapeDtypeStruct((AXES['h...  3.52 us
  transfers between devices with their start and end apart: 2, of which 2 were waited for; matrix products, arithmetic and copies ran while one was open for 0% of the time, Pallas kernels for 0%

profile of v4, /device:TPU:1, one launch (start us, length us, event | category | flops | bytes accessed | tf_op | source)
XLA Modules:
  0.0 135.4 jit_solution(4334729419891681708)
XLA Ops:
  0.0 0.0 copy-start.2
  0.0 11.9 %all_to_all.15.own = bf16[2,16,8192]{2,1,0:T(8,128)(2,1)S(1)} all-to-all(bf16[2,16,8192]{2,1,0:T(8,128)(2,1)} %bitcast.15), channel_id=1, replica_groups=mesh['y'=4,'half'=2,'x'=4,'z'=8,'core'=2] {'core'}, dimensions={0} | all-to-all | bytes 1048576 | tf_op jit(solution)/shard_map/all_to_all | solution.py:210
  11.9 9.7 %collective-permute-start.1 = (bf16[2,16,8192]{2,1,0:T(8,128)(2,1)S(1)}, bf16[2,16,8192]{2,1,0:T(8,128)(2,1)S(1)}, u32[]{:S(2)}, u32[]{:S(2)}) collective-permute-start(bf16[2,16,8192]{2,1,0:T(8,128)(2,1)S(1)} %all_to_all.15.own), channel_id=1, source_target_pairs={{0,62},{2,0},{4,2},{6,4},{8,6},{10,8},{12,10},{14,12},{16,14},{18,... | collective-permute-start | bytes 1572872 | tf_op jit(solution)/shard_map/ppermute | solution.py:211
  21.6 1.3 collective-permute-start
  22.9 0.0 copy-start
  22.9 2.2 %copy-done = bf16[2,1024,1024]{2,1,0:T(8,128)(2,1)S(1)} copy-done((bf16[2,1024,1024]{2,1,0:T(8,128)(2,1)S(1)}, bf16[2,1024,1024]{2,1,0:T(8,128)(2,1)}, u32[]{:S(2)}) %copy-start) | copy-done | bytes 4194328
  25.1 0.0 copy-start.1
  25.1 1.5 %copy-done.1 = bf16[32,30720]{1,0:T(8,128)(2,1)S(1)} copy-done((bf16[32,30720]{1,0:T(8,128)(2,1)S(1)}, bf16[32,30720]{1,0:T(8,128)(2,1)}, u32[]{:S(2)}) %copy-start.1) | copy-done | bytes 1966104
  26.6 0.6 shard_map.46
  27.2 0.1 pad_add_fusion.place_ref
  27.3 5.2 %collective-permute-done.1.right = bf16[2,16,8192]{2,1,0:T(8,128)(2,1)S(1)} collective-permute-done((bf16[2,16,8192]{2,1,0:T(8,128)(2,1)S(1)}, bf16[2,16,8192]{2,1,0:T(8,128)(2,1)S(1)}, u32[]{:S(2)}, u32[]{:S(2)}) %collective-permute-start.1) | collective-permute-done | bytes 524320 | tf_op jit(solution)/shard_map/ppermute | solution.py:211
  32.5 11.2 %collective-permute-done.left = bf16[2,16,8192]{2,1,0:T(8,128)(2,1)S(1)} collective-permute-done((bf16[2,16,8192]{2,1,0:T(8,128)(2,1)S(1)}, bf16[2,16,8192]{2,1,0:T(8,128)(2,1)S(1)}, u32[]{:S(2)}, u32[]{:S(2)}) %collective-permute-start) | collective-permute-done | bytes 524320 | tf_op jit(solution)/shard_map/ppermute | solution.py:212
  43.7 0.0 copy-done.2
  43.8 3.5 %shard_map.47 = bf16[2,2048,128]{2,1,0:T(8,128)(2,1)S(1)} custom-call(s32[3]{0:T(128)S(1)} %pad_add_fusion.place_ref, bf16[2,16,8192]{2,1,0:T(8,128)(2,1)S(1)} %collective-permute-done.left, bf16[2,16,8192]{2,1,0:T(8,128)(2,1)S(1)} %all_to_all.15.own, bf16[2,16,8192]{2,1,0:T(8,128)(2,1)S(1)} %collective-permute-done.1.right, ...), custom_call_target="tpu_custom_call" | custom-call | tf_op jit(solution)/shard_map/pallas_call | solution.py:137
  47.3 72.5 %all_to_all.16 = bf16[512,8,128]{2,1,0:T(8,128)(2,1)S(1)} all-to-all(bf16[512,8,128]{2,1,0:T(8,128)(2,1)S(1)} %bitcast.12), channel_id=1, replica_groups=mesh['y'=4,'half'=2,'x'=4,'z'=8,'core'=2] {'half','core','x','y','z'}, dimensions={0} | all-to-all | bytes 2097152 | tf_op jit(solution)/shard_map/all_to_all | solution.py:219
  119.7 0.1 copy.8
  119.9 0.3 copy.9
  120.2 2.0 %shard_map.48 = bf16[4,2,4,32,256]{4,3,2,1,0:T(8,128)(2,1)S(1)} custom-call(s32[3]{0:T(128)S(1)} %pad_add_fusion.place_ref, bf16[4,1024,128]{2,1,0:T(8,128)(2,1)S(1)} %bitcast.13), custom_call_target="tpu_custom_call" | custom-call | tf_op jit(solution)/shard_map/pallas_call | solution.py:195
  122.2 12.0 %all_to_all.17 = bf16[4,2,4,32,256]{4,3,2,1,0:T(8,128)(2,1)S(1)} all-to-all(bf16[4,2,4,32,256]{4,3,2,1,0:T(8,128)(2,1)S(1)} %shard_map.48), channel_id=1, replica_groups=mesh['y'=4,'half'=2,'x'=4,'z'=8,'core'=2] {'y'}, dimensions={0} | all-to-all | bytes 1048576 | tf_op jit(solution)/shard_map/all_to_all | solution.py:223
  134.2 0.1 convert_bitcast_fusion
  134.3 1.1 copy.10
Async XLA Ops:
  0.0 43.8 %copy-start.2 = (f32[16,2048]{1,0:T(8,128)S(1)}, f32[16,2048]{1,0:T(8,128)}, u32[]{:S(2)}) copy-start(f32[16,2048]{1,0:T(8,128)} %taps.1) | copy-start | bytes 393220
  11.9 20.7 %collective-permute-start.1 = (bf16[2,16,8192]{2,1,0:T(8,128)(2,1)S(1)}, bf16[2,16,8192]{2,1,0:T(8,128)(2,1)S(1)}, u32[]{:S(2)}, u32[]{:S(2)}) collective-permute-start(bf16[2,16,8192]{2,1,0:T(8,128)(2,1)S(1)} %all_to_all.15.own), channel_id=1, source_target_pairs={{0,62},{2,0},{4,2},{6,4},{8,6},{10,8},{12,10},{14,12},{16,14},{18,... | collective-permute-start | bytes 1572872 | tf_op jit(solution)/shard_map/ppermute | solution.py:211
  21.6 22.2 %collective-permute-start = (bf16[2,16,8192]{2,1,0:T(8,128)(2,1)S(1)}, bf16[2,16,8192]{2,1,0:T(8,128)(2,1)S(1)}, u32[]{:S(2)}, u32[]{:S(2)}) collective-permute-start(bf16[2,16,8192]{2,1,0:T(8,128)(2,1)S(1)} %all_to_all.15.own), channel_id=1, source_target_pairs={{0,2},{2,4},{4,6},{6,8},{8,10},{10,12},{12,14},{14,16},{16,18},{18... | collective-permute-start | bytes 1572872 | tf_op jit(solution)/shard_map/ppermute | solution.py:212
  22.9 2.2 %copy-start = (bf16[2,1024,1024]{2,1,0:T(8,128)(2,1)S(1)}, bf16[2,1024,1024]{2,1,0:T(8,128)(2,1)}, u32[]{:S(2)}) copy-start(bf16[2,1024,1024]{2,1,0:T(8,128)(2,1)} %constant.26.clone.table) | copy-start | bytes 12582916
  25.1 1.5 %copy-start.1 = (bf16[32,30720]{1,0:T(8,128)(2,1)S(1)}, bf16[32,30720]{1,0:T(8,128)(2,1)}, u32[]{:S(2)}) copy-start(bf16[32,30720]{1,0:T(8,128)(2,1)} %previous.1) | copy-start | bytes 5898244

commit v5 on v4

v5 whole, which is shorter than its diff:
```python
import functools
import math

import jax
import jax.numpy as jnp
import ml_dtypes
import numpy as np
from jax import lax
from jax.experimental import pallas as pl
from jax.experimental.pallas import tpu as pltpu
from jax.sharding import Mesh
from jax.sharding import PartitionSpec as P

FRAME = 2048
HALF = FRAME // 2
TAPS = 16
REACH = TAPS - 1
AHEAD = 8
STEPS = 2
VMEM_BYTES = 20 * 2**20
LOAD_BYTES = 12 * 2**20


AXES = {"y": 4, "half": 2, "x": 4, "z": 8, "core": 2}
FEED = ("y", "half")
TIME = ("x", "z", "core")
CHIP = ("x", "z")
ORDER = ("half", "core", "x", "y", "z")
CHANNELS = 4
BLOCK = AXES["z"] * CHANNELS * 2


def dft_table():
    parity = np.arange(2).reshape(2, 1, 1, 1, 1, 1)
    core = np.arange(2).reshape(1, 2, 1, 1, 1, 1)
    x = np.arange(4).reshape(1, 1, 4, 1, 1, 1)
    upper = np.arange(2).reshape(1, 1, 1, 2, 1, 1)
    z = np.arange(8).reshape(1, 1, 1, 1, 8, 1)
    own = np.arange(CHANNELS).reshape(1, 1, 1, 1, 1, CHANNELS)
    channel = ((x * 8 + z) * 2 + core) * 16 + own * 4 + upper * 2 + parity
    turns = (channel.reshape(-1, 1) * np.arange(FRAME // 2)[None, :]) % FRAME
    angle = turns * (2.0 * math.pi / FRAME)
    table = np.stack([np.cos(angle), -np.sin(angle)], axis=1)
    return table.reshape(2, HALF, FRAME // 2).astype(ml_dtypes.bfloat16)


def load_kernel(table, previous, table_here, previous_here, arrived):
    copies = (
        pltpu.make_async_copy(table, table_here, arrived.at[0]),
        pltpu.make_async_copy(previous, previous_here, arrived.at[1]),
    )
    for copy in copies:
        copy.start()
    for copy in copies:
        copy.wait()


def load(table, previous):
    on_chip = pl.BlockSpec(memory_space=pltpu.VMEM)
    return pl.pallas_call(
        load_kernel,
        out_shape=tuple(jax.ShapeDtypeStruct(a.shape, a.dtype) for a in (table, previous)),
        in_specs=[pl.BlockSpec(memory_space=pl.ANY)] * 2,
        out_specs=(on_chip, on_chip),
        scratch_shapes=[pltpu.SemaphoreType.DMA((2,))],
        compiler_params=pltpu.CompilerParams(vmem_limit_bytes=LOAD_BYTES),
    )(table, previous)


def channelize_kernel(place_ref, own, swapped, first, passed, second, previous, taps, table, out, folded):
    inputs, block = own.shape
    here = block // FRAME
    start = place_ref[0]

    def filter_frames(sources):
        def columns(j, carry):
            for row in range(0, inputs, 16):
                parts = []
                for part in range(2):
                    lane = pl.multiple_of(part * (FRAME // 2) + j * 128, 128)
                    weights = [taps[t : t + 1, pl.ds(lane, 128)] for t in range(TAPS)]
                    frames = []
                    for w in range(here + REACH):
                        source, frame = sources[(w + 1) // here], (w + 1) % here
                        at = pl.ds(pl.multiple_of(frame * FRAME + lane, 128), 128)
                        value = source[row : row + 16, at].astype(jnp.float32)
                        if w < REACH:
                            held = jnp.clip(start + w + REACH, 0, REACH - 1) * FRAME + lane
                            at = pl.ds(pl.multiple_of(held, 128), 128)
                            old = previous[row : row + 16, at].astype(jnp.float32)
                            value = jnp.where(start + w < 0, old, value)
                        frames.append(value)
                    totals = []
                    for s in range(here):
                        total = weights[0] * frames[s]
                        for t in range(1, TAPS):
                            total = total + weights[t] * frames[s + t]
                        totals.append(total)
                    parts.append(totals)
                at = pl.ds(pl.multiple_of(j * 128, 128), 128)
                for s, (low, high) in enumerate(zip(*parts)):
                    rows = pl.ds(s * inputs + row, 16)
                    folded[0, rows, at] = (low + high).astype(jnp.bfloat16)
                    folded[1, rows, at] = (low - high).astype(jnp.bfloat16)
            return carry

        lax.fori_loop(0, FRAME // 2 // 128, columns, 0)

    @pl.when(place_ref[1] == 0)
    def _():
        filter_frames((second, passed, own, swapped, first))

    @pl.when(place_ref[1] == 1)
    def _():
        filter_frames((first, swapped, own, passed, second))

    step = table.shape[1] // STEPS
    for parity in range(2):
        for j in range(STEPS):
            spectrum = lax.dot_general(
                table[parity, j * step : (j + 1) * step, :],
                folded[parity],
                (((1,), (1,)), ((), ())),
                preferred_element_type=jnp.float32,
            )
            spectrum = (spectrum * (1.0 / math.sqrt(FRAME))).astype(jnp.bfloat16)
            for block in range(step // BLOCK):
                row = ((j * (step // BLOCK) + block) * 2 + parity) * BLOCK
                for half in range(out.shape[0]):
                    out[half, row : row + BLOCK, :] = spectrum[block * BLOCK : (block + 1) * BLOCK]


def channelize(place, blocks, previous, taps, table):
    inputs, block = blocks[0].shape
    rows = inputs * (block // FRAME)
    on_chip = pl.BlockSpec(memory_space=pltpu.VMEM)
    operands = (*blocks, previous, taps, table)
    return pl.pallas_call(
        channelize_kernel,
        out_shape=jax.ShapeDtypeStruct((AXES["half"], 2 * table.shape[1], rows), jnp.bfloat16),
        in_specs=[pl.BlockSpec(memory_space=pltpu.SMEM)] + [on_chip] * len(operands),
        out_specs=on_chip,
        scratch_shapes=[pltpu.VMEM((2, rows, FRAME // 2), jnp.bfloat16)],
        compiler_params=pltpu.CompilerParams(vmem_limit_bytes=VMEM_BYTES),
    )(place, *operands)


def correlate_kernel(inputs, scale, place_ref, received, out, every, own):
    channels, rows, lanes = received.shape
    halves, count = AXES["half"], AXES["y"]
    wide = rows // (halves * count)
    sign = jnp.where(lax.broadcasted_iota(jnp.int32, (inputs, wide), 1) < wide // 2, 1.0, -1.0)
    for k in range(channels):
        for half in range(halves):
            for y in range(count):
                first = (half * count + y) * wide
                turned = received[k, first : first + wide, :].T
                row = (y * halves + half) * inputs
                for s in range(lanes // inputs):
                    at = slice(s * wide, (s + 1) * wide)
                    every[k, row : row + inputs, at] = turned[s * inputs : (s + 1) * inputs]
        for y in range(count):
            row = pl.multiple_of((y * halves + place_ref[2]) * inputs, inputs)
            for s in range(lanes // inputs):
                at = slice(s * wide, (s + 1) * wide)
                part = every[k, pl.ds(row, inputs), at]
                own[k, y * inputs : (y + 1) * inputs, at] = part
                part = pltpu.roll(part.astype(jnp.float32), wide // 2, 1) * sign
                own[k, (count + y) * inputs : (count + y + 1) * inputs, at] = part.astype(jnp.bfloat16)
    for k in range(channels):
        sums = lax.dot_general(
            own[k], every[k], (((1,), (1,)), ((), ())), preferred_element_type=jnp.float32
        )
        sums = (sums * scale).astype(jnp.bfloat16)
        for part in range(2):
            for y in range(count):
                row = (part * count + y) * inputs
                out[y, part, k] = sums[row : row + inputs]


def correlate(place, received, inputs, scale):
    channels, rows, lanes = received.shape
    count, total = AXES["y"], AXES["y"] * AXES["half"] * inputs
    depth = rows * lanes // total
    return pl.pallas_call(
        functools.partial(correlate_kernel, inputs, scale),
        out_shape=jax.ShapeDtypeStruct((count, 2, channels, inputs, total), jnp.bfloat16),
        in_specs=[pl.BlockSpec(memory_space=pltpu.SMEM), pl.BlockSpec(memory_space=pltpu.VMEM)],
        out_specs=pl.BlockSpec(memory_space=pltpu.VMEM),
        scratch_shapes=[pltpu.VMEM((channels, total, depth), jnp.bfloat16)] * 2,
        compiler_params=pltpu.CompilerParams(vmem_limit_bytes=32 * 2**20),
    )(place, received)


def widen_kernel(result, out, wide, sent):
    count, parts, channels = result.shape[:3]
    copies = []
    for part in range(parts):
        for k in range(channels):
            for y in range(count):
                wide[part, k * count + y] = result[y, part, k].astype(jnp.float32)
            at = pl.ds(k * count, count)
            copy = pltpu.make_async_copy(wide.at[part, at], out.at[part, at], sent.at[part * channels + k])
            copy.start()
            copies.append(copy)
    for copy in copies:
        copy.wait()


def widen(result):
    count, parts, channels, inputs, total = result.shape
    shape = (parts, channels * count, inputs, total)
    return pl.pallas_call(
        widen_kernel,
        out_shape=jax.ShapeDtypeStruct(shape, jnp.float32),
        in_specs=[pl.BlockSpec(memory_space=pltpu.VMEM)],
        out_specs=pl.BlockSpec(memory_space=pl.ANY),
        scratch_shapes=[pltpu.VMEM(shape, jnp.float32), pltpu.SemaphoreType.DMA((parts * channels,))],
        compiler_params=pltpu.CompilerParams(vmem_limit_bytes=16 * 2**20),
    )(result)


def body(table, voltages, previous, filter_taps):
    inputs, block = voltages.shape
    here = block // FRAME
    chips, cores = math.prod(AXES[a] for a in CHIP), AXES["core"]
    chip, core = lax.axis_index(CHIP), lax.axis_index("core")
    up = [(c, c + 1) for c in range(chips - 2)]
    down = [(c, (c - 1) % chips) for c in range(chips)]
    route = lambda steps, core: [(a * cores + core, b * cores + core) for a, b in steps]
    first = lax.ppermute(voltages, TIME, route(up, 1) + route(down, 0))
    second = lax.ppermute(voltages, TIME, route(up, 0) + route(down, 1))
    swapped = lax.ppermute(voltages, "core", [(0, 1), (1, 0)])
    passed = lax.ppermute(first, "core", [(0, 1), (1, 0)])
    table, old = load(table, previous)
    start = (chip * cores + core) * here + AHEAD - REACH - jnp.where(chip == chips - 1, chips * cores * here, 0)
    place = jnp.stack([start, core, lax.axis_index("half")]).astype(jnp.int32)
    spectra = channelize(place, (voltages, swapped, first, passed, second), old, filter_taps, table)
    rows = spectra.shape[2]
    devices = math.prod(AXES.values())
    received = lax.all_to_all(spectra.reshape(devices, CHANNELS * 2, rows), ORDER, 0, 0, tiled=True)
    received = received.reshape(*(AXES[a] for a in ORDER), CHANNELS, 2, rows)
    received = received.transpose(5, 0, 3, 6, 1, 2, 4, 7).reshape(CHANNELS, -1, rows)
    result = correlate(place, received, inputs, FRAME / (chips * cores * block))
    result = lax.all_to_all(result, "y", 0, 0, tiled=True)
    return widen(result)


def solution(mesh):
    parts = Mesh(mesh.devices.reshape(tuple(AXES.values())), tuple(AXES))
    table = dft_table()
    placed = (P(FEED, TIME), P(FEED, None), P())

    def run(voltages, previous, filter_taps):
        return jax.shard_map(
            functools.partial(body, jnp.asarray(table)),
            mesh=parts,
            in_specs=placed,
            out_specs=P(None, TIME, FEED, None),
            check_vma=False,
        )(voltages, previous, filter_taps)

    return run
```

time: 136 us -> 131 us (0.963)
  starting transfers between devices: 11 us -> 27.7 us
  waiting for transfers between devices: 16.4 us -> 0.64 us
  blocking collectives: 96.3 us -> 91.2 us
    ppermute x2 -> x4, starting transfers between devices: 11 us -> 27.7 us  [the longest x1 14.4 us: body(): swapped = lax.ppermute(voltages, 'core', [(0, 1), (1, 0)])]
    ppermute x2 -> x4, waiting for transfers between devices: 16.4 us -> 0.64 us  [the longest x1 0.63 us: body(): second = lax.ppermute(voltages, TIME, route(up, 0) + route(down, 1))]
    all_to_all x1 -> x0, blocking collectives: 11.9 us -> none  [body(): lax.all_to_all(voltages.reshape(CORES, here, block), 'core', 0, 0, tiled=...]
    all_to_all x1, blocking collectives: 72.5 us -> 79.1 us  [body(): lax.all_to_all(spectra.reshape(devices, CHANNELS * 2, rows), ORDER, 0, 0,...]
    unnamed x6 -> x8, local copies, waits for them, and re-layouts: 3.73 us -> 3.74 us
  transfers between devices with their start and end apart: 2 -> 4, of which waited for: 2 -> 1; matrix products, arithmetic and copies ran while one was open for 0% -> 0% of each run, Pallas kernels for 0% -> 0%
where the time goes in v5:
time: 131 us
  blocking collectives  91.2 us (70%)
  starting transfers between devices  27.7 us (21%)
  Pallas kernels  7.27 us (6%)
  local copies, waits for them, and re-layouts  4.16 us (3%)
    all_to_all x1, blocking collectives, body(): lax.all_to_all(spectra.reshape(devices, CHANNELS * 2, rows), ORDER, 0, 0,...  79.1 us
    ppermute x1, starting transfers between devices, body(): swapped = lax.ppermute(voltages, 'core', [(0, 1), (1, 0)])  14.4 us
    all_to_all x1, blocking collectives, body(): result = lax.all_to_all(result, 'y', 0, 0, tiled=True)  12 us
    ppermute x1, starting transfers between devices, body(): passed = lax.ppermute(first, 'core', [(0, 1), (1, 0)])  7.01 us
    ppermute x1, starting transfers between devices, body(): first = lax.ppermute(voltages, TIME, route(up, 1) + route(down, 0))  4.39 us
    pallas_call x1, Pallas kernels, channelize(): pl.pallas_call(channelize_kernel, out_shape=jax.ShapeDtypeStruct((AXES['h...  4.2 us
    unnamed x8, local copies, waits for them, and re-layouts  3.74 us
  transfers between devices with their start and end apart: 4, of which 1 were waited for; matrix products, arithmetic and copies ran while one was open for 0% of the time, Pallas kernels for 0%

profile of v5, /device:TPU:1, one launch (start us, length us, event | category | flops | bytes accessed | tf_op | source)
XLA Modules:
  0.0 131.1 jit_solution(16091907317346025409)
XLA Ops:
  0.0 4.4 %collective-permute-start.1 = (bf16[32,8192]{1,0:T(8,128)(2,1)}, bf16[32,8192]{1,0:T(8,128)(2,1)S(1)}, u32[]{:S(2)}, u32[]{:S(2)}) collective-permute-start(bf16[32,8192]{1,0:T(8,128)(2,1)} %own.1), channel_id=1, source_target_pairs={{1,3},{3,5},{5,7},{7,9},{9,11},{11,13},{13,15},{15,17},{17,19},{19... | collective-permute-start | bytes 1572872 | tf_op jit(solution)/shard_map/ppermute | solution.py:231
  4.4 14.4 %collective-permute-start = (bf16[32,8192]{1,0:T(8,128)(2,1)}, bf16[32,8192]{1,0:T(8,128)(2,1)S(1)}, u32[]{:S(2)}, u32[]{:S(2)}) collective-permute-start(bf16[32,8192]{1,0:T(8,128)(2,1)} %own.1), channel_id=1, source_target_pairs={{0,1},{1,0},{2,3},{3,2},{4,5},{5,4},{6,7},{7,6},{8,9},{9,8},{10,11... | collective-permute-start | bytes 1572872 | tf_op jit(solution)/shard_map/ppermute | solution.py:233
  18.8 1.9 %collective-permute-start.3 = (bf16[32,8192]{1,0:T(8,128)(2,1)}, bf16[32,8192]{1,0:T(8,128)(2,1)S(1)}, u32[]{:S(2)}, u32[]{:S(2)}) collective-permute-start(bf16[32,8192]{1,0:T(8,128)(2,1)} %own.1), channel_id=1, source_target_pairs={{0,2},{2,4},{4,6},{6,8},{8,10},{10,12},{12,14},{14,16},{16,18},{18... | collective-permute-start | bytes 1572872 | tf_op jit(solution)/shard_map/ppermute | solution.py:232
  20.7 0.0 collective-permute-done.1.first
  20.7 7.0 %collective-permute-start.2 = (bf16[32,8192]{1,0:T(8,128)(2,1)S(1)}, bf16[32,8192]{1,0:T(8,128)(2,1)S(1)}, u32[]{:S(2)}, u32[]{:S(2)}) collective-permute-start(bf16[32,8192]{1,0:T(8,128)(2,1)S(1)} %collective-permute-done.1.first), channel_id=1, source_target_pairs={{0,1},{1,0},{2,3},{3,2},{4,5},{5,4},{6,7},{7,6},{8,9},{9,8},{10,11... | collective-permute-start | bytes 1572872 | tf_op jit(solution)/shard_map/ppermute | solution.py:234
  27.7 0.0 copy-start
  27.8 2.2 %copy-done = bf16[2,1024,1024]{2,1,0:T(8,128)(2,1)S(1)} copy-done((bf16[2,1024,1024]{2,1,0:T(8,128)(2,1)S(1)}, bf16[2,1024,1024]{2,1,0:T(8,128)(2,1)}, u32[]{:S(2)}) %copy-start) | copy-done | bytes 4194328
  29.9 0.0 copy-start.1
  29.9 1.5 %copy-done.1 = bf16[32,30720]{1,0:T(8,128)(2,1)S(1)} copy-done((bf16[32,30720]{1,0:T(8,128)(2,1)S(1)}, bf16[32,30720]{1,0:T(8,128)(2,1)}, u32[]{:S(2)}) %copy-start.1) | copy-done | bytes 1966104
  31.5 0.0 copy-start.2
  31.5 0.0 copy-start.3
  31.5 0.6 shard_map.46
  32.1 0.1 pad_add_fusion.place_ref
  32.2 0.0 collective-permute-done.swapped
  32.2 0.6 collective-permute-done.3.second
  32.8 0.0 collective-permute-done.2.passed
  32.8 0.0 copy-done.2
  32.8 0.0 copy-done.3
  32.8 4.2 %shard_map.47 = bf16[2,2048,128]{2,1,0:T(8,128)(2,1)S(1)} custom-call(s32[3]{0:T(128)S(1)} %pad_add_fusion.place_ref, bf16[32,8192]{1,0:T(8,128)(2,1)S(1)} %copy-done.2, bf16[32,8192]{1,0:T(8,128)(2,1)S(1)} %collective-permute-done.swapped, bf16[32,8192]{1,0:T(8,128)(2,1)S(1)} %collective-permute-done.1.first, ...), custom_call_target="tpu_custom_call" | custom-call | tf_op jit(solution)/shard_map/pallas_call | solution.py:138
  37.0 79.1 %all_to_all.10 = bf16[512,8,128]{2,1,0:T(8,128)(2,1)S(1)} all-to-all(bf16[512,8,128]{2,1,0:T(8,128)(2,1)S(1)} %bitcast.8), channel_id=1, replica_groups=mesh['y'=4,'half'=2,'x'=4,'z'=8,'core'=2] {'half','core','x','y','z'}, dimensions={0} | all-to-all | bytes 2097152 | tf_op jit(solution)/shard_map/all_to_all | solution.py:241
  116.2 0.1 copy.7
  116.3 0.3 copy.8
  116.6 1.4 %shard_map.48 = bf16[4,2,4,32,256]{4,3,2,1,0:T(8,128)(2,1)S(1)} custom-call(s32[3]{0:T(128)S(1)} %pad_add_fusion.place_ref, bf16[4,1024,128]{2,1,0:T(8,128)(2,1)S(1)} %bitcast.9), custom_call_target="tpu_custom_call" | custom-call | tf_op jit(solution)/shard_map/pallas_call | solution.py:185
  118.1 12.0 %all_to_all.11.result = bf16[4,2,4,32,256]{4,3,2,1,0:T(8,128)(2,1)S(1)} all-to-all(bf16[4,2,4,32,256]{4,3,2,1,0:T(8,128)(2,1)S(1)} %shard_map.48), channel_id=1, replica_groups=mesh['y'=4,'half'=2,'x'=4,'z'=8,'core'=2] {'y'}, dimensions={0} | all-to-all | bytes 1048576 | tf_op jit(solution)/shard_map/all_to_all | solution.py:245
  130.1 1.0 shard_map.49
Async XLA Ops:
  0.0 20.7 %collective-permute-start.1 = (bf16[32,8192]{1,0:T(8,128)(2,1)}, bf16[32,8192]{1,0:T(8,128)(2,1)S(1)}, u32[]{:S(2)}, u32[]{:S(2)}) collective-permute-start(bf16[32,8192]{1,0:T(8,128)(2,1)} %own.1), channel_id=1, source_target_pairs={{1,3},{3,5},{5,7},{7,9},{9,11},{11,13},{13,15},{15,17},{17,19},{19... | collective-permute-start | bytes 1572872 | tf_op jit(solution)/shard_map/ppermute | solution.py:231
  4.4 27.8 %collective-permute-start = (bf16[32,8192]{1,0:T(8,128)(2,1)}, bf16[32,8192]{1,0:T(8,128)(2,1)S(1)}, u32[]{:S(2)}, u32[]{:S(2)}) collective-permute-start(bf16[32,8192]{1,0:T(8,128)(2,1)} %own.1), channel_id=1, source_target_pairs={{0,1},{1,0},{2,3},{3,2},{4,5},{5,4},{6,7},{7,6},{8,9},{9,8},{10,11... | collective-permute-start | bytes 1572872 | tf_op jit(solution)/shard_map/ppermute | solution.py:233
  18.8 14.0 %collective-permute-start.3 = (bf16[32,8192]{1,0:T(8,128)(2,1)}, bf16[32,8192]{1,0:T(8,128)(2,1)S(1)}, u32[]{:S(2)}, u32[]{:S(2)}) collective-permute-start(bf16[32,8192]{1,0:T(8,128)(2,1)} %own.1), channel_id=1, source_target_pairs={{0,2},{2,4},{4,6},{6,8},{8,10},{10,12},{12,14},{14,16},{16,18},{18... | collective-permute-start | bytes 1572872 | tf_op jit(solution)/shard_map/ppermute | solution.py:232
  20.7 12.1 %collective-permute-start.2 = (bf16[32,8192]{1,0:T(8,128)(2,1)S(1)}, bf16[32,8192]{1,0:T(8,128)(2,1)S(1)}, u32[]{:S(2)}, u32[]{:S(2)}) collective-permute-start(bf16[32,8192]{1,0:T(8,128)(2,1)S(1)} %collective-permute-done.1.first), channel_id=1, source_target_pairs={{0,1},{1,0},{2,3},{3,2},{4,5},{5,4},{6,7},{7,6},{8,9},{9,8},{10,11... | collective-permute-start | bytes 1572872 | tf_op jit(solution)/shard_map/ppermute | solution.py:234
  27.7 2.2 %copy-start = (bf16[2,1024,1024]{2,1,0:T(8,128)(2,1)S(1)}, bf16[2,1024,1024]{2,1,0:T(8,128)(2,1)}, u32[]{:S(2)}) copy-start(bf16[2,1024,1024]{2,1,0:T(8,128)(2,1)} %constant.36.clone.table) | copy-start | bytes 12582916
  29.9 1.5 %copy-start.1 = (bf16[32,30720]{1,0:T(8,128)(2,1)S(1)}, bf16[32,30720]{1,0:T(8,128)(2,1)}, u32[]{:S(2)}) copy-start(bf16[32,30720]{1,0:T(8,128)(2,1)} %previous.1) | copy-start | bytes 5898244
  31.5 1.3 %copy-start.2 = (bf16[32,8192]{1,0:T(8,128)(2,1)S(1)}, bf16[32,8192]{1,0:T(8,128)(2,1)}, u32[]{:S(2)}) copy-start(bf16[32,8192]{1,0:T(8,128)(2,1)} %own.1) | copy-start | bytes 1572868
  31.5 1.3 %copy-start.3 = (f32[16,2048]{1,0:T(8,128)S(1)}, f32[16,2048]{1,0:T(8,128)}, u32[]{:S(2)}) copy-start(f32[16,2048]{1,0:T(8,128)} %taps.1) | copy-start | bytes 393220

commit v6 on v5

--- a/solution.py
+++ b/solution.py
@@ -73,6 +73,8 @@
     start = place_ref[0]
 
     def filter_frames(sources):
+        held = [jnp.clip(start + w + REACH, 0, REACH - 1) * FRAME for w in range(REACH)]
+
         def columns(j, carry):
             for row in range(0, inputs, 16):
                 parts = []
@@ -85,8 +87,7 @@
                         at = pl.ds(pl.multiple_of(frame * FRAME + lane, 128), 128)
                         value = source[row : row + 16, at].astype(jnp.float32)
                         if w < REACH:
-                            held = jnp.clip(start + w + REACH, 0, REACH - 1) * FRAME + lane
-                            at = pl.ds(pl.multiple_of(held, 128), 128)
+                            at = pl.ds(pl.multiple_of(held[w] + lane, 128), 128)
                             old = previous[row : row + 16, at].astype(jnp.float32)
                             value = jnp.where(start + w < 0, old, value)
                         frames.append(value)
@@ -230,8 +231,9 @@
     route = lambda steps, core: [(a * cores + core, b * cores + core) for a, b in steps]
     first = lax.ppermute(voltages, TIME, route(up, 1) + route(down, 0))
     second = lax.ppermute(voltages, TIME, route(up, 0) + route(down, 1))
-    swapped = lax.ppermute(voltages, "core", [(0, 1), (1, 0)])
+    mine, first = lax.optimization_barrier((voltages, first))
     passed = lax.ppermute(first, "core", [(0, 1), (1, 0)])
+    swapped = lax.ppermute(mine, "core", [(0, 1), (1, 0)])
     table, old = load(table, previous)
     start = (chip * cores + core) * here + AHEAD - REACH - jnp.where(chip == chips - 1, chips * cores * here, 0)
     place = jnp.stack([start, core, lax.axis_index("half")]).astype(jnp.int32)

time: 131 us -> 135 us (1.031)
  starting transfers between devices: 27.7 us -> 32.9 us
  blocking collectives: 91.2 us -> 89.8 us
    ppermute x1, starting transfers between devices: 1.92 us -> 12.2 us  [body(): second = lax.ppermute(voltages, TIME, route(up, 0) + route(down, 1))]
    ppermute x1, starting transfers between devices: 7.01 us -> 1.92 us  [body(): passed = lax.ppermute(first, 'core', [(0, 1), (1, 0)])]
  transfers between devices with their start and end apart: 4 -> 4, of which waited for: 1 -> 0; matrix products, arithmetic and copies ran while one was open for 0% -> 0% of each run, Pallas kernels for 0% -> 0%
where the time goes in v6:
time: 135 us
  blocking collectives  89.8 us (67%)
  starting transfers between devices  32.9 us (24%)
  Pallas kernels  7.21 us (5%)
  local copies, waits for them, and re-layouts  4.52 us (3%)
    all_to_all x1, blocking collectives, body(): lax.all_to_all(spectra.reshape(devices, CHANNELS * 2, rows), ORDER, 0, 0,...  77.9 us
    ppermute x1, starting transfers between devices, body(): swapped = lax.ppermute(mine, 'core', [(0, 1), (1, 0)])  14.4 us
    ppermute x1, starting transfers between devices, body(): second = lax.ppermute(voltages, TIME, route(up, 0) + route(down, 1))  12.2 us
    all_to_all x1, blocking collectives, body(): result = lax.all_to_all(result, 'y', 0, 0, tiled=True)  12 us
    ppermute x1, starting transfers between devices, body(): first = lax.ppermute(voltages, TIME, route(up, 1) + route(down, 0))  4.39 us
    pallas_call x1, Pallas kernels, channelize(): pl.pallas_call(channelize_kernel, out_shape=jax.ShapeDtypeStruct((AXES['h...  4.13 us
    unnamed x8, local copies, waits for them, and re-layouts  4.1 us
  transfers between devices with their start and end apart: 4, of which 0 were waited for; matrix products, arithmetic and copies ran while one was open for 0% of the time, Pallas kernels for 0%

profile of v6, /device:TPU:1, one launch (start us, length us, event | category | flops | bytes accessed | tf_op | source)
XLA Modules:
  0.0 134.6 jit_solution(5996306732819206754)
XLA Ops:
  0.0 4.4 %collective-permute-start = (bf16[32,8192]{1,0:T(8,128)(2,1)}, bf16[32,8192]{1,0:T(8,128)(2,1)S(1)}, u32[]{:S(2)}, u32[]{:S(2)}) collective-permute-start(bf16[32,8192]{1,0:T(8,128)(2,1)} %own.1), channel_id=1, source_target_pairs={{1,3},{3,5},{5,7},{7,9},{9,11},{11,13},{13,15},{15,17},{17,19},{19... | collective-permute-start | bytes 1572872 | tf_op jit(solution)/shard_map/ppermute | solution.py:232
  4.4 12.2 %collective-permute-start.3 = (bf16[32,8192]{1,0:T(8,128)(2,1)}, bf16[32,8192]{1,0:T(8,128)(2,1)S(1)}, u32[]{:S(2)}, u32[]{:S(2)}) collective-permute-start(bf16[32,8192]{1,0:T(8,128)(2,1)} %own.1), channel_id=1, source_target_pairs={{0,2},{2,4},{4,6},{6,8},{8,10},{10,12},{12,14},{14,16},{16,18},{18... | collective-permute-start | bytes 1572872 | tf_op jit(solution)/shard_map/ppermute | solution.py:233
  16.6 0.0 collective-permute-done.first
  16.6 14.4 %collective-permute-start.1 = (bf16[32,8192]{1,0:T(8,128)(2,1)}, bf16[32,8192]{1,0:T(8,128)(2,1)S(1)}, u32[]{:S(2)}, u32[]{:S(2)}) collective-permute-start(bf16[32,8192]{1,0:T(8,128)(2,1)} %own.1), channel_id=1, source_target_pairs={{0,1},{1,0},{2,3},{3,2},{4,5},{5,4},{6,7},{7,6},{8,9},{9,8},{10,11... | collective-permute-start | bytes 1572872 | tf_op jit(solution)/shard_map/ppermute | solution.py:236
  31.0 1.9 %collective-permute-start.2 = (bf16[32,8192]{1,0:T(8,128)(2,1)S(1)}, bf16[32,8192]{1,0:T(8,128)(2,1)S(1)}, u32[]{:S(2)}, u32[]{:S(2)}) collective-permute-start(bf16[32,8192]{1,0:T(8,128)(2,1)S(1)} %collective-permute-done.first), channel_id=1, source_target_pairs={{0,1},{1,0},{2,3},{3,2},{4,5},{5,4},{6,7},{7,6},{8,9},{9,8},{10,11... | collective-permute-start | bytes 1572872 | tf_op jit(solution)/shard_map/ppermute | solution.py:235
  32.9 0.0 copy-start
  32.9 2.2 %copy-done = bf16[2,1024,1024]{2,1,0:T(8,128)(2,1)S(1)} copy-done((bf16[2,1024,1024]{2,1,0:T(8,128)(2,1)S(1)}, bf16[2,1024,1024]{2,1,0:T(8,128)(2,1)}, u32[]{:S(2)}) %copy-start) | copy-done | bytes 4194328
  35.1 0.0 copy-start.1
  35.1 1.5 %copy-done.1 = bf16[32,30720]{1,0:T(8,128)(2,1)S(1)} copy-done((bf16[32,30720]{1,0:T(8,128)(2,1)S(1)}, bf16[32,30720]{1,0:T(8,128)(2,1)}, u32[]{:S(2)}) %copy-start.1) | copy-done | bytes 1966104
  36.7 0.0 copy-start.2
  36.7 0.0 copy-start.3
  36.7 0.6 shard_map.46
  37.3 0.1 pad_add_fusion.place_ref
  37.3 0.0 collective-permute-done.3.second
  37.4 0.0 collective-permute-done.1.swapped
  37.4 0.0 collective-permute-done.2.passed
  37.4 0.3 copy-done.2
  37.7 0.0 copy-done.3
  37.7 4.1 %shard_map.47 = bf16[2,2048,128]{2,1,0:T(8,128)(2,1)S(1)} custom-call(s32[3]{0:T(128)S(1)} %pad_add_fusion.place_ref, bf16[32,8192]{1,0:T(8,128)(2,1)S(1)} %copy-done.2, bf16[32,8192]{1,0:T(8,128)(2,1)S(1)} %collective-permute-done.1.swapped, bf16[32,8192]{1,0:T(8,128)(2,1)S(1)} %collective-permute-done.first, ...), custom_call_target="tpu_custom_call" | custom-call | tf_op jit(solution)/shard_map/pallas_call | solution.py:139
  41.9 77.9 %all_to_all.10 = bf16[512,8,128]{2,1,0:T(8,128)(2,1)S(1)} all-to-all(bf16[512,8,128]{2,1,0:T(8,128)(2,1)S(1)} %bitcast.8), channel_id=1, replica_groups=mesh['y'=4,'half'=2,'x'=4,'z'=8,'core'=2] {'half','core','x','y','z'}, dimensions={0} | all-to-all | bytes 2097152 | tf_op jit(solution)/shard_map/all_to_all | solution.py:243
  119.7 0.1 copy.7
  119.9 0.3 copy.8
  120.2 1.5 %shard_map.48 = bf16[4,2,4,32,256]{4,3,2,1,0:T(8,128)(2,1)S(1)} custom-call(s32[3]{0:T(128)S(1)} %pad_add_fusion.place_ref, bf16[4,1024,128]{2,1,0:T(8,128)(2,1)S(1)} %bitcast.9), custom_call_target="tpu_custom_call" | custom-call | tf_op jit(solution)/shard_map/pallas_call | solution.py:186
  121.6 12.0 %all_to_all.11.result = bf16[4,2,4,32,256]{4,3,2,1,0:T(8,128)(2,1)S(1)} all-to-all(bf16[4,2,4,32,256]{4,3,2,1,0:T(8,128)(2,1)S(1)} %shard_map.48), channel_id=1, replica_groups=mesh['y'=4,'half'=2,'x'=4,'z'=8,'core'=2] {'y'}, dimensions={0} | all-to-all | bytes 1048576 | tf_op jit(solution)/shard_map/all_to_all | solution.py:247
  133.6 1.0 shard_map.49
Async XLA Ops:
  0.0 16.6 %collective-permute-start = (bf16[32,8192]{1,0:T(8,128)(2,1)}, bf16[32,8192]{1,0:T(8,128)(2,1)S(1)}, u32[]{:S(2)}, u32[]{:S(2)}) collective-permute-start(bf16[32,8192]{1,0:T(8,128)(2,1)} %own.1), channel_id=1, source_target_pairs={{1,3},{3,5},{5,7},{7,9},{9,11},{11,13},{13,15},{15,17},{17,19},{19... | collective-permute-start | bytes 1572872 | tf_op jit(solution)/shard_map/ppermute | solution.py:232
  4.4 33.0 %collective-permute-start.3 = (bf16[32,8192]{1,0:T(8,128)(2,1)}, bf16[32,8192]{1,0:T(8,128)(2,1)S(1)}, u32[]{:S(2)}, u32[]{:S(2)}) collective-permute-start(bf16[32,8192]{1,0:T(8,128)(2,1)} %own.1), channel_id=1, source_target_pairs={{0,2},{2,4},{4,6},{6,8},{8,10},{10,12},{12,14},{14,16},{16,18},{18... | collective-permute-start | bytes 1572872 | tf_op jit(solution)/shard_map/ppermute | solution.py:233
  16.6 20.7 %collective-permute-start.1 = (bf16[32,8192]{1,0:T(8,128)(2,1)}, bf16[32,8192]{1,0:T(8,128)(2,1)S(1)}, u32[]{:S(2)}, u32[]{:S(2)}) collective-permute-start(bf16[32,8192]{1,0:T(8,128)(2,1)} %own.1), channel_id=1, source_target_pairs={{0,1},{1,0},{2,3},{3,2},{4,5},{5,4},{6,7},{7,6},{8,9},{9,8},{10,11... | collective-permute-start | bytes 1572872 | tf_op jit(solution)/shard_map/ppermute | solution.py:236
  31.0 6.4 %collective-permute-start.2 = (bf16[32,8192]{1,0:T(8,128)(2,1)S(1)}, bf16[32,8192]{1,0:T(8,128)(2,1)S(1)}, u32[]{:S(2)}, u32[]{:S(2)}) collective-permute-start(bf16[32,8192]{1,0:T(8,128)(2,1)S(1)} %collective-permute-done.first), channel_id=1, source_target_pairs={{0,1},{1,0},{2,3},{3,2},{4,5},{5,4},{6,7},{7,6},{8,9},{9,8},{10,11... | collective-permute-start | bytes 1572872 | tf_op jit(solution)/shard_map/ppermute | solution.py:235
  32.9 2.2 %copy-start = (bf16[2,1024,1024]{2,1,0:T(8,128)(2,1)S(1)}, bf16[2,1024,1024]{2,1,0:T(8,128)(2,1)}, u32[]{:S(2)}) copy-start(bf16[2,1024,1024]{2,1,0:T(8,128)(2,1)} %constant.36.clone.table) | copy-start | bytes 12582916
  35.1 1.5 %copy-start.1 = (bf16[32,30720]{1,0:T(8,128)(2,1)S(1)}, bf16[32,30720]{1,0:T(8,128)(2,1)}, u32[]{:S(2)}) copy-start(bf16[32,30720]{1,0:T(8,128)(2,1)} %previous.1) | copy-start | bytes 5898244
  36.7 1.0 copy-start.2
  36.7 1.1 copy-start.3

commit v7 on v6

--- a/solution.py
+++ b/solution.py
@@ -17,8 +17,8 @@
 REACH = TAPS - 1
 AHEAD = 8
 STEPS = 2
-VMEM_BYTES = 20 * 2**20
-LOAD_BYTES = 12 * 2**20
+VMEM_BYTES = 50 * 2**20
+LOAD_BYTES = 4 * 2**20
 
 
 AXES = {"y": 4, "half": 2, "x": 4, "z": 8, "core": 2}
@@ -44,10 +44,10 @@
     return table.reshape(2, HALF, FRAME // 2).astype(ml_dtypes.bfloat16)
 
 
-def load_kernel(table, previous, table_here, previous_here, arrived):
+def load_kernel(voltages, taps, voltages_here, taps_here, arrived):
     copies = (
-        pltpu.make_async_copy(table, table_here, arrived.at[0]),
-        pltpu.make_async_copy(previous, previous_here, arrived.at[1]),
+        pltpu.make_async_copy(voltages, voltages_here, arrived.at[0]),
+        pltpu.make_async_copy(taps, taps_here, arrived.at[1]),
     )
     for copy in copies:
         copy.start()
@@ -55,22 +55,30 @@
         copy.wait()
 
 
-def load(table, previous):
+def load(voltages, taps):
     on_chip = pl.BlockSpec(memory_space=pltpu.VMEM)
     return pl.pallas_call(
         load_kernel,
-        out_shape=tuple(jax.ShapeDtypeStruct(a.shape, a.dtype) for a in (table, previous)),
+        out_shape=tuple(jax.ShapeDtypeStruct(a.shape, a.dtype) for a in (voltages, taps)),
         in_specs=[pl.BlockSpec(memory_space=pl.ANY)] * 2,
         out_specs=(on_chip, on_chip),
         scratch_shapes=[pltpu.SemaphoreType.DMA((2,))],
         compiler_params=pltpu.CompilerParams(vmem_limit_bytes=LOAD_BYTES),
-    )(table, previous)
-
-
-def channelize_kernel(place_ref, own, swapped, first, passed, second, previous, taps, table, out, folded):
+    )(voltages, taps)
+
+
+def channelize_kernel(place_ref, own, swapped, first, passed, second, taps, far_previous, far_table, out, folded, previous, table, arrived):
     inputs, block = own.shape
     here = block // FRAME
     start = place_ref[0]
+    table_copy = pltpu.make_async_copy(far_table, table, arrived.at[0])
+    table_copy.start()
+
+    @pl.when(start < 0)
+    def _():
+        copy = pltpu.make_async_copy(far_previous, previous, arrived.at[1])
+        copy.start()
+        copy.wait()
 
     def filter_frames(sources):
         held = [jnp.clip(start + w + REACH, 0, REACH - 1) * FRAME for w in range(REACH)]
@@ -115,6 +123,7 @@
     def _():
         filter_frames((first, swapped, own, passed, second))
 
+    table_copy.wait()
     step = table.shape[1] // STEPS
     for parity in range(2):
         for j in range(STEPS):
@@ -135,15 +144,19 @@
     inputs, block = blocks[0].shape
     rows = inputs * (block // FRAME)
     on_chip = pl.BlockSpec(memory_space=pltpu.VMEM)
-    operands = (*blocks, previous, taps, table)
+    near, far = (*blocks, taps), (previous, table)
     return pl.pallas_call(
         channelize_kernel,
         out_shape=jax.ShapeDtypeStruct((AXES["half"], 2 * table.shape[1], rows), jnp.bfloat16),
-        in_specs=[pl.BlockSpec(memory_space=pltpu.SMEM)] + [on_chip] * len(operands),
+        in_specs=[pl.BlockSpec(memory_space=pltpu.SMEM)]
+        + [on_chip] * len(near)
+        + [pl.BlockSpec(memory_space=pltpu.HBM)] * len(far),
         out_specs=on_chip,
-        scratch_shapes=[pltpu.VMEM((2, rows, FRAME // 2), jnp.bfloat16)],
+        scratch_shapes=[pltpu.VMEM((2, rows, FRAME // 2), jnp.bfloat16)]
+        + [pltpu.VMEM(a.shape, a.dtype) for a in far]
+        + [pltpu.SemaphoreType.DMA((len(far),))],
         compiler_params=pltpu.CompilerParams(vmem_limit_bytes=VMEM_BYTES),
-    )(place, *operands)
+    )(place, *near, *far)
 
 
 def correlate_kernel(inputs, scale, place_ref, received, out, every, own):
@@ -234,10 +247,10 @@
     mine, first = lax.optimization_barrier((voltages, first))
     passed = lax.ppermute(first, "core", [(0, 1), (1, 0)])
     swapped = lax.ppermute(mine, "core", [(0, 1), (1, 0)])
-    table, old = load(table, previous)
     start = (chip * cores + core) * here + AHEAD - REACH - jnp.where(chip == chips - 1, chips * cores * here, 0)
     place = jnp.stack([start, core, lax.axis_index("half")]).astype(jnp.int32)
-    spectra = channelize(place, (voltages, swapped, first, passed, second), old, filter_taps, table)
+    own, taps = load(voltages, filter_taps)
+    spectra = channelize(place, (own, swapped, first, passed, second), previous, taps, table)
     rows = spectra.shape[2]
     devices = math.prod(AXES.values())
     received = lax.all_to_all(spectra.reshape(devices, CHANNELS * 2, rows), ORDER, 0, 0, tiled=True)

time: 135 us -> 132 us (0.978)
  blocking collectives: 89.8 us -> 87.1 us
  Pallas kernels: 7.21 us -> 9.63 us
  local copies, waits for them, and re-layouts: 4.52 us -> 2.36 us
    pallas_call x1, Pallas kernels: 4.13 us -> 6.93 us  [channelize(): pl.pallas_call(channelize_kernel, out_shape=jax.ShapeDtypeStruct((AXES['h...]
    all_to_all x1, blocking collectives: 77.9 us -> 75.1 us  [body(): lax.all_to_all(spectra.reshape(devices, CHANNELS * 2, rows), ORDER, 0, 0,...]
    unnamed x8 -> x4, local copies, waits for them, and re-layouts: 4.1 us -> 1.94 us
where the time goes in v7:
time: 132 us
  blocking collectives  87.1 us (66%)
  starting transfers between devices  32.9 us (25%)
  Pallas kernels  9.63 us (7%)
  local copies, waits for them, and re-layouts  2.36 us (2%)
    all_to_all x1, blocking collectives, body(): lax.all_to_all(spectra.reshape(devices, CHANNELS * 2, rows), ORDER, 0, 0,...  75.1 us
    ppermute x1, starting transfers between devices, body(): swapped = lax.ppermute(mine, 'core', [(0, 1), (1, 0)])  14.4 us
    ppermute x1, starting transfers between devices, body(): second = lax.ppermute(voltages, TIME, route(up, 0) + route(down, 1))  12.2 us
    all_to_all x1, blocking collectives, body(): result = lax.all_to_all(result, 'y', 0, 0, tiled=True)  12 us
    pallas_call x1, Pallas kernels, channelize(): pl.pallas_call(channelize_kernel, out_shape=jax.ShapeDtypeStruct((AXES['h...  6.93 us
    ppermute x1, starting transfers between devices, body(): first = lax.ppermute(voltages, TIME, route(up, 1) + route(down, 0))  4.39 us
  transfers between devices with their start and end apart: 4, of which 0 were waited for; matrix products, arithmetic and copies ran while one was open for 0% of the time, Pallas kernels for 0%

profile of v7, /device:TPU:1, one launch (start us, length us, event | category | flops | bytes accessed | tf_op | source)
XLA Modules:
  0.0 132.2 jit_solution(14362384818510334546)
XLA Ops:
  0.0 4.4 %collective-permute-start = (bf16[32,8192]{1,0:T(8,128)(2,1)}, bf16[32,8192]{1,0:T(8,128)(2,1)S(1)}, u32[]{:S(2)}, u32[]{:S(2)}) collective-permute-start(bf16[32,8192]{1,0:T(8,128)(2,1)} %voltages.1), channel_id=1, source_target_pairs={{1,3},{3,5},{5,7},{7,9},{9,11},{11,13},{13,15},{15,17},{17,19},{19... | collective-permute-start | bytes 1572872 | tf_op jit(solution)/shard_map/ppermute | solution.py:245
  4.4 12.2 %collective-permute-start.3 = (bf16[32,8192]{1,0:T(8,128)(2,1)}, bf16[32,8192]{1,0:T(8,128)(2,1)S(1)}, u32[]{:S(2)}, u32[]{:S(2)}) collective-permute-start(bf16[32,8192]{1,0:T(8,128)(2,1)} %voltages.1), channel_id=1, source_target_pairs={{0,2},{2,4},{4,6},{6,8},{8,10},{10,12},{12,14},{14,16},{16,18},{18... | collective-permute-start | bytes 1572872 | tf_op jit(solution)/shard_map/ppermute | solution.py:246
  16.6 0.0 collective-permute-done.first
  16.6 14.4 %collective-permute-start.1 = (bf16[32,8192]{1,0:T(8,128)(2,1)}, bf16[32,8192]{1,0:T(8,128)(2,1)S(1)}, u32[]{:S(2)}, u32[]{:S(2)}) collective-permute-start(bf16[32,8192]{1,0:T(8,128)(2,1)} %voltages.1), channel_id=1, source_target_pairs={{0,1},{1,0},{2,3},{3,2},{4,5},{5,4},{6,7},{7,6},{8,9},{9,8},{10,11... | collective-permute-start | bytes 1572872 | tf_op jit(solution)/shard_map/ppermute | solution.py:249
  31.0 1.9 %collective-permute-start.2 = (bf16[32,8192]{1,0:T(8,128)(2,1)S(1)}, bf16[32,8192]{1,0:T(8,128)(2,1)S(1)}, u32[]{:S(2)}, u32[]{:S(2)}) collective-permute-start(bf16[32,8192]{1,0:T(8,128)(2,1)S(1)} %collective-permute-done.first), channel_id=1, source_target_pairs={{0,1},{1,0},{2,3},{3,2},{4,5},{5,4},{6,7},{7,6},{8,9},{9,8},{10,11... | collective-permute-start | bytes 1572872 | tf_op jit(solution)/shard_map/ppermute | solution.py:248
  32.9 0.0 copy-start
  32.9 1.0 copy-done
  34.0 0.0 copy-start.1
  34.0 0.9 copy-done.1
  34.9 0.2 shard_map.46
  35.1 0.1 pad_add_fusion.place_ref
  35.2 0.0 collective-permute-done.3.second
  35.2 0.0 collective-permute-done.1.swapped
  35.2 0.0 collective-permute-done.2.passed
  35.2 6.9 %shard_map.47 = bf16[2,2048,128]{2,1,0:T(8,128)(2,1)S(1)} custom-call(s32[3]{0:T(128)S(1)} %pad_add_fusion.place_ref, bf16[32,8192]{1,0:T(8,128)(2,1)S(1)} %get-tuple-element.9.own, bf16[32,8192]{1,0:T(8,128)(2,1)S(1)} %collective-permute-done.1.swapped, bf16[32,8192]{1,0:T(8,128)(2,1)S(1)} %collective-permute-done.first, ...), custom_call_target="tpu_custom_call" | custom-call | tf_op jit(solution)/shard_map/pallas_call | solution.py:148
  42.1 75.1 %all_to_all.10 = bf16[512,8,128]{2,1,0:T(8,128)(2,1)S(1)} all-to-all(bf16[512,8,128]{2,1,0:T(8,128)(2,1)S(1)} %bitcast.8), channel_id=1, replica_groups=mesh['y'=4,'half'=2,'x'=4,'z'=8,'core'=2] {'half','core','x','y','z'}, dimensions={0} | all-to-all | bytes 2097152 | tf_op jit(solution)/shard_map/all_to_all | solution.py:256
  117.2 0.1 copy.7
  117.4 0.3 copy.8
  117.7 1.4 %shard_map.48 = bf16[4,2,4,32,256]{4,3,2,1,0:T(8,128)(2,1)S(1)} custom-call(s32[3]{0:T(128)S(1)} %pad_add_fusion.place_ref, bf16[4,1024,128]{2,1,0:T(8,128)(2,1)S(1)} %bitcast.9), custom_call_target="tpu_custom_call" | custom-call | tf_op jit(solution)/shard_map/pallas_call | solution.py:199
  119.1 12.0 %all_to_all.11.result = bf16[4,2,4,32,256]{4,3,2,1,0:T(8,128)(2,1)S(1)} all-to-all(bf16[4,2,4,32,256]{4,3,2,1,0:T(8,128)(2,1)S(1)} %shard_map.48), channel_id=1, replica_groups=mesh['y'=4,'half'=2,'x'=4,'z'=8,'core'=2] {'y'}, dimensions={0} | all-to-all | bytes 1048576 | tf_op jit(solution)/shard_map/all_to_all | solution.py:260
  131.1 1.0 shard_map.49
Async XLA Ops:
  0.0 16.6 %collective-permute-start = (bf16[32,8192]{1,0:T(8,128)(2,1)}, bf16[32,8192]{1,0:T(8,128)(2,1)S(1)}, u32[]{:S(2)}, u32[]{:S(2)}) collective-permute-start(bf16[32,8192]{1,0:T(8,128)(2,1)} %voltages.1), channel_id=1, source_target_pairs={{1,3},{3,5},{5,7},{7,9},{9,11},{11,13},{13,15},{15,17},{17,19},{19... | collective-permute-start | bytes 1572872 | tf_op jit(solution)/shard_map/ppermute | solution.py:245
  4.4 30.8 %collective-permute-start.3 = (bf16[32,8192]{1,0:T(8,128)(2,1)}, bf16[32,8192]{1,0:T(8,128)(2,1)S(1)}, u32[]{:S(2)}, u32[]{:S(2)}) collective-permute-start(bf16[32,8192]{1,0:T(8,128)(2,1)} %voltages.1), channel_id=1, source_target_pairs={{0,2},{2,4},{4,6},{6,8},{8,10},{10,12},{12,14},{14,16},{16,18},{18... | collective-permute-start | bytes 1572872 | tf_op jit(solution)/shard_map/ppermute | solution.py:246
  16.6 18.6 %collective-permute-start.1 = (bf16[32,8192]{1,0:T(8,128)(2,1)}, bf16[32,8192]{1,0:T(8,128)(2,1)S(1)}, u32[]{:S(2)}, u32[]{:S(2)}) collective-permute-start(bf16[32,8192]{1,0:T(8,128)(2,1)} %voltages.1), channel_id=1, source_target_pairs={{0,1},{1,0},{2,3},{3,2},{4,5},{5,4},{6,7},{7,6},{8,9},{9,8},{10,11... | collective-permute-start | bytes 1572872 | tf_op jit(solution)/shard_map/ppermute | solution.py:249
  31.0 4.2 %collective-permute-start.2 = (bf16[32,8192]{1,0:T(8,128)(2,1)S(1)}, bf16[32,8192]{1,0:T(8,128)(2,1)S(1)}, u32[]{:S(2)}, u32[]{:S(2)}) collective-permute-start(bf16[32,8192]{1,0:T(8,128)(2,1)S(1)} %collective-permute-done.first), channel_id=1, source_target_pairs={{0,1},{1,0},{2,3},{3,2},{4,5},{5,4},{6,7},{7,6},{8,9},{9,8},{10,11... | collective-permute-start | bytes 1572872 | tf_op jit(solution)/shard_map/ppermute | solution.py:248
  32.9 1.0 copy-start
  34.0 0.9 copy-start.1

commit v8 on v7

--- a/solution.py
+++ b/solution.py
@@ -44,41 +44,39 @@
     return table.reshape(2, HALF, FRAME // 2).astype(ml_dtypes.bfloat16)
 
 
-def load_kernel(voltages, taps, voltages_here, taps_here, arrived):
-    copies = (
-        pltpu.make_async_copy(voltages, voltages_here, arrived.at[0]),
-        pltpu.make_async_copy(taps, taps_here, arrived.at[1]),
-    )
+def load_kernel(count, *refs):
+    copies = [pltpu.make_async_copy(refs[i], refs[count + i], refs[-1].at[i]) for i in range(count)]
     for copy in copies:
         copy.start()
     for copy in copies:
         copy.wait()
 
 
-def load(voltages, taps):
-    on_chip = pl.BlockSpec(memory_space=pltpu.VMEM)
-    return pl.pallas_call(
-        load_kernel,
-        out_shape=tuple(jax.ShapeDtypeStruct(a.shape, a.dtype) for a in (voltages, taps)),
-        in_specs=[pl.BlockSpec(memory_space=pl.ANY)] * 2,
-        out_specs=(on_chip, on_chip),
-        scratch_shapes=[pltpu.SemaphoreType.DMA((2,))],
+def load(*arrays):
+    count = len(arrays)
+    return pl.pallas_call(
+        functools.partial(load_kernel, count),
+        out_shape=tuple(jax.ShapeDtypeStruct(a.shape, a.dtype) for a in arrays),
+        in_specs=[pl.BlockSpec(memory_space=pl.ANY)] * count,
+        out_specs=(pl.BlockSpec(memory_space=pltpu.VMEM),) * count,
+        scratch_shapes=[pltpu.SemaphoreType.DMA((count,))],
         compiler_params=pltpu.CompilerParams(vmem_limit_bytes=LOAD_BYTES),
-    )(voltages, taps)
+    )(*arrays)
 
 
 def channelize_kernel(place_ref, own, swapped, first, passed, second, taps, far_previous, far_table, out, folded, previous, table, arrived):
     inputs, block = own.shape
     here = block // FRAME
     start = place_ref[0]
-    table_copy = pltpu.make_async_copy(far_table, table, arrived.at[0])
-    table_copy.start()
 
     @pl.when(start < 0)
     def _():
         copy = pltpu.make_async_copy(far_previous, previous, arrived.at[1])
         copy.start()
         copy.wait()
+
+    table_copy = pltpu.make_async_copy(far_table, table, arrived.at[0])
+    table_copy.start()
 
     def filter_frames(sources):
         held = [jnp.clip(start + w + REACH, 0, REACH - 1) * FRAME for w in range(REACH)]
@@ -244,12 +242,11 @@
     route = lambda steps, core: [(a * cores + core, b * cores + core) for a, b in steps]
     first = lax.ppermute(voltages, TIME, route(up, 1) + route(down, 0))
     second = lax.ppermute(voltages, TIME, route(up, 0) + route(down, 1))
-    mine, first = lax.optimization_barrier((voltages, first))
+    own, taps = load(voltages, filter_taps)
+    swapped = lax.ppermute(own, "core", [(0, 1), (1, 0)])
     passed = lax.ppermute(first, "core", [(0, 1), (1, 0)])
-    swapped = lax.ppermute(mine, "core", [(0, 1), (1, 0)])
     start = (chip * cores + core) * here + AHEAD - REACH - jnp.where(chip == chips - 1, chips * cores * here, 0)
     place = jnp.stack([start, core, lax.axis_index("half")]).astype(jnp.int32)
-    own, taps = load(voltages, filter_taps)
     spectra = channelize(place, (own, swapped, first, passed, second), previous, taps, table)
     rows = spectra.shape[2]
     devices = math.prod(AXES.values())

time: 132 us -> 131 us (level)
  starting transfers between devices: 32.9 us -> 28.8 us
  blocking collectives: 87.1 us -> 89.2 us
  waiting for transfers between devices: 0.01 us -> 1.43 us
    ppermute x1, starting transfers between devices: 14.4 us -> 3.5 us  [body(): swapped = lax.ppermute(own, 'core', [(0, 1), (1, 0)])]
    ppermute x1, starting transfers between devices: 1.92 us -> 8.67 us  [body(): passed = lax.ppermute(first, 'core', [(0, 1), (1, 0)])]
    all_to_all x1, blocking collectives: 75.1 us -> 77.2 us  [body(): lax.all_to_all(spectra.reshape(devices, CHANNELS * 2, rows), ORDER, 0, 0,...]
    ppermute x1, waiting for transfers between devices: 0.01 us -> 1.42 us  [body(): passed = lax.ppermute(first, 'core', [(0, 1), (1, 0)])]
  transfers between devices with their start and end apart: 4 -> 4, of which waited for: 0 -> 1; matrix products, arithmetic and copies ran while one was open for 0% -> 0% of each run, Pallas kernels for 0% -> 0%
where the time goes in v8:
time: 131 us; the launch traced here: 130 us
  blocking collectives  89.2 us (68%)
  starting transfers between devices  28.8 us (22%)
  Pallas kernels  8.36 us (6%)
  local copies, waits for them, and re-layouts  2.37 us (2%)
  waiting for transfers between devices  1.43 us (1%)
    all_to_all x1, blocking collectives, body(): lax.all_to_all(spectra.reshape(devices, CHANNELS * 2, rows), ORDER, 0, 0,...  77.2 us
    ppermute x1, starting transfers between devices, body(): second = lax.ppermute(voltages, TIME, route(up, 0) + route(down, 1))  12.2 us
    all_to_all x1, blocking collectives, body(): result = lax.all_to_all(result, 'y', 0, 0, tiled=True)  12 us
    ppermute x1, starting transfers between devices, body(): passed = lax.ppermute(first, 'core', [(0, 1), (1, 0)])  8.67 us
    pallas_call x1, Pallas kernels, channelize(): pl.pallas_call(channelize_kernel, out_shape=jax.ShapeDtypeStruct((AXES['h...  5.65 us
    ppermute x1, starting transfers between devices, body(): first = lax.ppermute(voltages, TIME, route(up, 1) + route(down, 0))  4.39 us
    ppermute x1, starting transfers between devices, body(): swapped = lax.ppermute(own, 'core', [(0, 1), (1, 0)])  3.5 us
  transfers between devices with their start and end apart: 4, of which 1 were waited for; matrix products, arithmetic and copies ran while one was open for 0% of the time, Pallas kernels for 0%

profile of v8, /device:TPU:1, one launch (start us, length us, event | category | flops | bytes accessed | tf_op | source)
XLA Modules:
  0.0 130.3 jit_solution(4347908654994174514)
XLA Ops:
  0.0 4.4 %collective-permute-start.1 = (bf16[32,8192]{1,0:T(8,128)(2,1)}, bf16[32,8192]{1,0:T(8,128)(2,1)S(1)}, u32[]{:S(2)}, u32[]{:S(2)}) collective-permute-start(bf16[32,8192]{1,0:T(8,128)(2,1)} %refs_0_.1), channel_id=1, source_target_pairs={{1,3},{3,5},{5,7},{7,9},{9,11},{11,13},{13,15},{15,17},{17,19},{19... | collective-permute-start | bytes 1572872 | tf_op jit(solution)/shard_map/ppermute | solution.py:243
  4.4 12.2 %collective-permute-start.3 = (bf16[32,8192]{1,0:T(8,128)(2,1)}, bf16[32,8192]{1,0:T(8,128)(2,1)S(1)}, u32[]{:S(2)}, u32[]{:S(2)}) collective-permute-start(bf16[32,8192]{1,0:T(8,128)(2,1)} %refs_0_.1), channel_id=1, source_target_pairs={{0,2},{2,4},{4,6},{6,8},{8,10},{10,12},{12,14},{14,16},{16,18},{18... | collective-permute-start | bytes 1572872 | tf_op jit(solution)/shard_map/ppermute | solution.py:244
  16.6 0.0 copy-start
  16.6 1.0 copy-done
  17.7 0.0 copy-start.1
  17.7 0.9 copy-done.1
  18.6 0.2 shard_map.46
  18.8 3.5 %collective-permute-start = (bf16[32,8192]{1,0:T(8,128)(2,1)S(1)}, bf16[32,8192]{1,0:T(8,128)(2,1)S(1)}, u32[]{:S(2)}, u32[]{:S(2)}) collective-permute-start(bf16[32,8192]{1,0:T(8,128)(2,1)S(1)} %get-tuple-element.7.own), channel_id=1, source_target_pairs={{0,1},{1,0},{2,3},{3,2},{4,5},{5,4},{6,7},{7,6},{8,9},{9,8},{10,11... | collective-permute-start | bytes 1572872 | tf_op jit(solution)/shard_map/ppermute | solution.py:246
  22.3 0.0 collective-permute-done.1.first
  22.3 8.7 %collective-permute-start.2 = (bf16[32,8192]{1,0:T(8,128)(2,1)S(1)}, bf16[32,8192]{1,0:T(8,128)(2,1)S(1)}, u32[]{:S(2)}, u32[]{:S(2)}) collective-permute-start(bf16[32,8192]{1,0:T(8,128)(2,1)S(1)} %collective-permute-done.1.first), channel_id=1, source_target_pairs={{0,1},{1,0},{2,3},{3,2},{4,5},{5,4},{6,7},{7,6},{8,9},{9,8},{10,11... | collective-permute-start | bytes 1572872 | tf_op jit(solution)/shard_map/ppermute | solution.py:247
  31.0 0.1 pad_add_fusion.place_ref
  31.1 0.0 collective-permute-done.3.second
  31.1 0.0 collective-permute-done.swapped
  31.1 1.4 %collective-permute-done.2.passed = bf16[32,8192]{1,0:T(8,128)(2,1)S(1)} collective-permute-done((bf16[32,8192]{1,0:T(8,128)(2,1)S(1)}, bf16[32,8192]{1,0:T(8,128)(2,1)S(1)}, u32[]{:S(2)}, u32[]{:S(2)}) %collective-permute-start.2) | collective-permute-done | bytes 524320 | tf_op jit(solution)/shard_map/ppermute | solution.py:247
  32.5 5.7 %shard_map.47 = bf16[2,2048,128]{2,1,0:T(8,128)(2,1)S(1)} custom-call(s32[3]{0:T(128)S(1)} %pad_add_fusion.place_ref, bf16[32,8192]{1,0:T(8,128)(2,1)S(1)} %get-tuple-element.7.own, bf16[32,8192]{1,0:T(8,128)(2,1)S(1)} %collective-permute-done.swapped, bf16[32,8192]{1,0:T(8,128)(2,1)S(1)} %collective-permute-done.1.first, ...), custom_call_target="tpu_custom_call" | custom-call | tf_op jit(solution)/shard_map/pallas_call | solution.py:146
  38.2 77.2 %all_to_all.10 = bf16[512,8,128]{2,1,0:T(8,128)(2,1)S(1)} all-to-all(bf16[512,8,128]{2,1,0:T(8,128)(2,1)S(1)} %bitcast.8), channel_id=1, replica_groups=mesh['y'=4,'half'=2,'x'=4,'z'=8,'core'=2] {'half','core','x','y','z'}, dimensions={0} | all-to-all | bytes 2097152 | tf_op jit(solution)/shard_map/all_to_all | solution.py:253
  115.3 0.1 copy.7
  115.5 0.3 copy.8
  115.8 1.5 %shard_map.48 = bf16[4,2,4,32,256]{4,3,2,1,0:T(8,128)(2,1)S(1)} custom-call(s32[3]{0:T(128)S(1)} %pad_add_fusion.place_ref, bf16[4,1024,128]{2,1,0:T(8,128)(2,1)S(1)} %bitcast.9), custom_call_target="tpu_custom_call" | custom-call | tf_op jit(solution)/shard_map/pallas_call | solution.py:197
  117.2 12.0 %all_to_all.11.result = bf16[4,2,4,32,256]{4,3,2,1,0:T(8,128)(2,1)S(1)} all-to-all(bf16[4,2,4,32,256]{4,3,2,1,0:T(8,128)(2,1)S(1)} %shard_map.48), channel_id=1, replica_groups=mesh['y'=4,'half'=2,'x'=4,'z'=8,'core'=2] {'y'}, dimensions={0} | all-to-all | bytes 1048576 | tf_op jit(solution)/shard_map/all_to_all | solution.py:257
  129.2 1.0 shard_map.49
Async XLA Ops:
  0.0 22.3 %collective-permute-start.1 = (bf16[32,8192]{1,0:T(8,128)(2,1)}, bf16[32,8192]{1,0:T(8,128)(2,1)S(1)}, u32[]{:S(2)}, u32[]{:S(2)}) collective-permute-start(bf16[32,8192]{1,0:T(8,128)(2,1)} %refs_0_.1), channel_id=1, source_target_pairs={{1,3},{3,5},{5,7},{7,9},{9,11},{11,13},{13,15},{15,17},{17,19},{19... | collective-permute-start | bytes 1572872 | tf_op jit(solution)/shard_map/ppermute | solution.py:243
  4.4 26.7 %collective-permute-start.3 = (bf16[32,8192]{1,0:T(8,128)(2,1)}, bf16[32,8192]{1,0:T(8,128)(2,1)S(1)}, u32[]{:S(2)}, u32[]{:S(2)}) collective-permute-start(bf16[32,8192]{1,0:T(8,128)(2,1)} %refs_0_.1), channel_id=1, source_target_pairs={{0,2},{2,4},{4,6},{6,8},{8,10},{10,12},{12,14},{14,16},{16,18},{18... | collective-permute-start | bytes 1572872 | tf_op jit(solution)/shard_map/ppermute | solution.py:244
  16.6 1.1 copy-start
  17.7 0.9 copy-start.1
  18.8 12.3 %collective-permute-start = (bf16[32,8192]{1,0:T(8,128)(2,1)S(1)}, bf16[32,8192]{1,0:T(8,128)(2,1)S(1)}, u32[]{:S(2)}, u32[]{:S(2)}) collective-permute-start(bf16[32,8192]{1,0:T(8,128)(2,1)S(1)} %get-tuple-element.7.own), channel_id=1, source_target_pairs={{0,1},{1,0},{2,3},{3,2},{4,5},{5,4},{6,7},{7,6},{8,9},{9,8},{10,11... | collective-permute-start | bytes 1572872 | tf_op jit(solution)/shard_map/ppermute | solution.py:246
  22.3 10.2 %collective-permute-start.2 = (bf16[32,8192]{1,0:T(8,128)(2,1)S(1)}, bf16[32,8192]{1,0:T(8,128)(2,1)S(1)}, u32[]{:S(2)}, u32[]{:S(2)}) collective-permute-start(bf16[32,8192]{1,0:T(8,128)(2,1)S(1)} %collective-permute-done.1.first), channel_id=1, source_target_pairs={{0,1},{1,0},{2,3},{3,2},{4,5},{5,4},{6,7},{7,6},{8,9},{9,8},{10,11... | collective-permute-start | bytes 1572872 | tf_op jit(solution)/shard_map/ppermute | solution.py:247

commit v9 on v8

--- a/solution.py
+++ b/solution.py
@@ -30,18 +30,21 @@
 BLOCK = AXES["z"] * CHANNELS * 2
 
 
-def dft_table():
-    parity = np.arange(2).reshape(2, 1, 1, 1, 1, 1)
-    core = np.arange(2).reshape(1, 2, 1, 1, 1, 1)
-    x = np.arange(4).reshape(1, 1, 4, 1, 1, 1)
-    upper = np.arange(2).reshape(1, 1, 1, 2, 1, 1)
-    z = np.arange(8).reshape(1, 1, 1, 1, 8, 1)
-    own = np.arange(CHANNELS).reshape(1, 1, 1, 1, 1, CHANNELS)
-    channel = ((x * 8 + z) * 2 + core) * 16 + own * 4 + upper * 2 + parity
-    turns = (channel.reshape(-1, 1) * np.arange(FRAME // 2)[None, :]) % FRAME
-    angle = turns * (2.0 * math.pi / FRAME)
-    table = np.stack([np.cos(angle), -np.sin(angle)], axis=1)
-    return table.reshape(2, HALF, FRAME // 2).astype(ml_dtypes.bfloat16)
+def dft_tables():
+    core = np.arange(2).reshape(2, 1, 1, 1, 1, 1)
+    x = np.arange(4).reshape(1, 4, 1, 1, 1, 1)
+    upper = np.arange(2).reshape(1, 1, 2, 1, 1, 1)
+    z = np.arange(8).reshape(1, 1, 1, 8, 1, 1)
+    own = np.arange(CHANNELS).reshape(1, 1, 1, 1, CHANNELS, 1)
+    even = ((x * 8 + z) * 2 + core) * 16 + own * 4 + upper * 2
+
+    def table(channel, count):
+        angle = channel * np.arange(count) % FRAME * (2.0 * math.pi / FRAME)
+        return np.stack([np.cos(angle), -np.sin(angle)], axis=-2).astype(ml_dtypes.bfloat16)
+
+    odd_table = table(even + 1, FRAME // 2).reshape(HALF, FRAME // 2)
+    even_table = np.moveaxis(table(even, FRAME // 4), 2, 0).reshape(2, HALF // 2, FRAME // 4)
+    return odd_table, even_table
 
 
 def load_kernel(count, *refs):
@@ -64,7 +67,7 @@
     )(*arrays)
 
 
-def channelize_kernel(place_ref, own, swapped, first, passed, second, taps, far_previous, far_table, out, folded, previous, table, arrived):
+def channelize_kernel(place_ref, own, swapped, first, passed, second, taps, far_previous, far_odd, far_even, out, folded, previous, odd, even, arrived):
     inputs, block = own.shape
     here = block // FRAME
     start = place_ref[0]
@@ -75,8 +78,10 @@
         copy.start()
         copy.wait()
 
-    table_copy = pltpu.make_async_copy(far_table, table, arrived.at[0])
-    table_copy.start()
+    odd_copy = pltpu.make_async_copy(far_odd, odd, arrived.at[0])
+    even_copy = pltpu.make_async_copy(far_even, even, arrived.at[2])
+    odd_copy.start()
+    even_copy.start()
 
     def filter_frames(sources):
         held = [jnp.clip(start + w + REACH, 0, REACH - 1) * FRAME for w in range(REACH)]
@@ -84,8 +89,8 @@
         def columns(j, carry):
             for row in range(0, inputs, 16):
                 parts = []
-                for part in range(2):
-                    lane = pl.multiple_of(part * (FRAME // 2) + j * 128, 128)
+                for part in range(4):
+                    lane = pl.multiple_of(part * (FRAME // 4) + j * 128, 128)
                     weights = [taps[t : t + 1, pl.ds(lane, 128)] for t in range(TAPS)]
                     frames = []
                     for w in range(here + REACH):
@@ -104,14 +109,17 @@
                             total = total + weights[t] * frames[s + t]
                         totals.append(total)
                     parts.append(totals)
-                at = pl.ds(pl.multiple_of(j * 128, 128), 128)
-                for s, (low, high) in enumerate(zip(*parts)):
+                at, later = (pl.ds(pl.multiple_of(j * 128 + k * FRAME // 4, 128), 128) for k in range(2))
+                for s, (first, second, third, fourth) in enumerate(zip(*parts)):
                     rows = pl.ds(s * inputs + row, 16)
-                    folded[0, rows, at] = (low + high).astype(jnp.bfloat16)
-                    folded[1, rows, at] = (low - high).astype(jnp.bfloat16)
+                    folded[1, rows, at] = (first - third).astype(jnp.bfloat16)
+                    folded[1, rows, later] = (second - fourth).astype(jnp.bfloat16)
+                    first, second = first + third, second + fourth
+                    folded[0, rows, at] = (first + second).astype(jnp.bfloat16)
+                    folded[0, rows, later] = (first - second).astype(jnp.bfloat16)
             return carry
 
-        lax.fori_loop(0, FRAME // 2 // 128, columns, 0)
+        lax.fori_loop(0, FRAME // 4 // 128, columns, 0)
 
     @pl.when(place_ref[1] == 0)
     def _():
@@ -121,31 +129,36 @@
     def _():
         filter_frames((first, swapped, own, passed, second))
 
-    table_copy.wait()
-    step = table.shape[1] // STEPS
-    for parity in range(2):
-        for j in range(STEPS):
-            spectrum = lax.dot_general(
-                table[parity, j * step : (j + 1) * step, :],
-                folded[parity],
-                (((1,), (1,)), ((), ())),
-                preferred_element_type=jnp.float32,
-            )
-            spectrum = (spectrum * (1.0 / math.sqrt(FRAME))).astype(jnp.bfloat16)
-            for block in range(step // BLOCK):
-                row = ((j * (step // BLOCK) + block) * 2 + parity) * BLOCK
-                for half in range(out.shape[0]):
-                    out[half, row : row + BLOCK, :] = spectrum[block * BLOCK : (block + 1) * BLOCK]
-
-
-def channelize(place, blocks, previous, taps, table):
+    def transform(table, frames):
+        spectrum = lax.dot_general(
+            table, frames, (((1,), (1,)), ((), ())), preferred_element_type=jnp.float32
+        )
+        return (spectrum * (1.0 / math.sqrt(FRAME))).astype(jnp.bfloat16)
+
+    def put(spectrum, first, stride):
+        for block in range(spectrum.shape[0] // BLOCK):
+            row = (first + block * stride) * BLOCK
+            for half in range(out.shape[0]):
+                out[half, row : row + BLOCK, :] = spectrum[block * BLOCK : (block + 1) * BLOCK]
+
+    odd_copy.wait()
+    even_copy.wait()
+    step = HALF // STEPS
+    for j in range(STEPS):
+        put(transform(odd[j * step : (j + 1) * step, :], folded[1]), j * step // BLOCK * 2 + 1, 2)
+    for upper in range(2):
+        at = slice(upper * FRAME // 4, (upper + 1) * FRAME // 4)
+        put(transform(even[upper], folded[0, :, at]), upper * 2, 4)
+
+
+def channelize(place, blocks, previous, taps, tables):
     inputs, block = blocks[0].shape
     rows = inputs * (block // FRAME)
     on_chip = pl.BlockSpec(memory_space=pltpu.VMEM)
-    near, far = (*blocks, taps), (previous, table)
+    near, far = (*blocks, taps), (previous, *tables)
     return pl.pallas_call(
         channelize_kernel,
-        out_shape=jax.ShapeDtypeStruct((AXES["half"], 2 * table.shape[1], rows), jnp.bfloat16),
+        out_shape=jax.ShapeDtypeStruct((AXES["half"], 2 * HALF, rows), jnp.bfloat16),
         in_specs=[pl.BlockSpec(memory_space=pltpu.SMEM)]
         + [on_chip] * len(near)
         + [pl.BlockSpec(memory_space=pltpu.HBM)] * len(far),
@@ -232,7 +245,7 @@
     )(result)
 
 
-def body(table, voltages, previous, filter_taps):
+def body(tables, voltages, previous, filter_taps):
     inputs, block = voltages.shape
     here = block // FRAME
     chips, cores = math.prod(AXES[a] for a in CHIP), AXES["core"]
@@ -247,7 +260,7 @@
     passed = lax.ppermute(first, "core", [(0, 1), (1, 0)])
     start = (chip * cores + core) * here + AHEAD - REACH - jnp.where(chip == chips - 1, chips * cores * here, 0)
     place = jnp.stack([start, core, lax.axis_index("half")]).astype(jnp.int32)
-    spectra = channelize(place, (own, swapped, first, passed, second), previous, taps, table)
+    spectra = channelize(place, (own, swapped, first, passed, second), previous, taps, tables)
     rows = spectra.shape[2]
     devices = math.prod(AXES.values())
     received = lax.all_to_all(spectra.reshape(devices, CHANNELS * 2, rows), ORDER, 0, 0, tiled=True)
@@ -260,12 +273,12 @@
 
 def solution(mesh):
     parts = Mesh(mesh.devices.reshape(tuple(AXES.values())), tuple(AXES))
-    table = dft_table()
+    tables = dft_tables()
     placed = (P(FEED, TIME), P(FEED, None), P())
 
     def run(voltages, previous, filter_taps):
         return jax.shard_map(
-            functools.partial(body, jnp.asarray(table)),
+            functools.partial(body, tuple(jnp.asarray(table) for table in tables)),
             mesh=parts,
             in_specs=placed,
             out_specs=P(None, TIME, FEED, None),

time: 131 us -> 130 us (level)
  no operation moved by 1% of the time
where the time goes in v9:
time: 130 us
  blocking collectives  89.2 us (69%)
  starting transfers between devices  28.8 us (22%)
  Pallas kernels  7.98 us (6%)
  local copies, waits for them, and re-layouts  2.37 us (2%)
  waiting for transfers between devices  1.43 us (1%)
    all_to_all x1, blocking collectives, body(): lax.all_to_all(spectra.reshape(devices, CHANNELS * 2, rows), ORDER, 0, 0,...  77.2 us
    ppermute x1, starting transfers between devices, body(): second = lax.ppermute(voltages, TIME, route(up, 0) + route(down, 1))  12.2 us
    all_to_all x1, blocking collectives, body(): result = lax.all_to_all(result, 'y', 0, 0, tiled=True)  12 us
    ppermute x1, starting transfers between devices, body(): passed = lax.ppermute(first, 'core', [(0, 1), (1, 0)])  8.67 us
    pallas_call x1, Pallas kernels, channelize(): pl.pallas_call(channelize_kernel, out_shape=jax.ShapeDtypeStruct((AXES['h...  5.27 us
    ppermute x1, starting transfers between devices, body(): first = lax.ppermute(voltages, TIME, route(up, 1) + route(down, 0))  4.39 us
    ppermute x1, starting transfers between devices, body(): swapped = lax.ppermute(own, 'core', [(0, 1), (1, 0)])  3.5 us
  transfers between devices with their start and end apart: 4, of which 1 were waited for; matrix products, arithmetic and copies ran while one was open for 0% of the time, Pallas kernels for 0%

profile of v9, /device:TPU:1, one launch (start us, length us, event | category | flops | bytes accessed | tf_op | source)
XLA Modules:
  0.0 129.9 jit_solution(10616442317542148767)
XLA Ops:
  0.0 4.4 %collective-permute-start.1 = (bf16[32,8192]{1,0:T(8,128)(2,1)}, bf16[32,8192]{1,0:T(8,128)(2,1)S(1)}, u32[]{:S(2)}, u32[]{:S(2)}) collective-permute-start(bf16[32,8192]{1,0:T(8,128)(2,1)} %refs_0_.1), channel_id=1, source_target_pairs={{1,3},{3,5},{5,7},{7,9},{9,11},{11,13},{13,15},{15,17},{17,19},{19... | collective-permute-start | bytes 1572872 | tf_op jit(solution)/shard_map/ppermute | solution.py:256
  4.4 12.2 %collective-permute-start.3 = (bf16[32,8192]{1,0:T(8,128)(2,1)}, bf16[32,8192]{1,0:T(8,128)(2,1)S(1)}, u32[]{:S(2)}, u32[]{:S(2)}) collective-permute-start(bf16[32,8192]{1,0:T(8,128)(2,1)} %refs_0_.1), channel_id=1, source_target_pairs={{0,2},{2,4},{4,6},{6,8},{8,10},{10,12},{12,14},{14,16},{16,18},{18... | collective-permute-start | bytes 1572872 | tf_op jit(solution)/shard_map/ppermute | solution.py:257
  16.6 0.0 copy-start
  16.6 1.0 copy-done
  17.7 0.0 copy-start.1
  17.7 0.9 copy-done.1
  18.6 0.2 shard_map.55
  18.8 3.5 %collective-permute-start = (bf16[32,8192]{1,0:T(8,128)(2,1)S(1)}, bf16[32,8192]{1,0:T(8,128)(2,1)S(1)}, u32[]{:S(2)}, u32[]{:S(2)}) collective-permute-start(bf16[32,8192]{1,0:T(8,128)(2,1)S(1)} %get-tuple-element.7.own), channel_id=1, source_target_pairs={{0,1},{1,0},{2,3},{3,2},{4,5},{5,4},{6,7},{7,6},{8,9},{9,8},{10,11... | collective-permute-start | bytes 1572872 | tf_op jit(solution)/shard_map/ppermute | solution.py:259
  22.3 0.0 collective-permute-done.1.first
  22.3 8.7 %collective-permute-start.2 = (bf16[32,8192]{1,0:T(8,128)(2,1)S(1)}, bf16[32,8192]{1,0:T(8,128)(2,1)S(1)}, u32[]{:S(2)}, u32[]{:S(2)}) collective-permute-start(bf16[32,8192]{1,0:T(8,128)(2,1)S(1)} %collective-permute-done.1.first), channel_id=1, source_target_pairs={{0,1},{1,0},{2,3},{3,2},{4,5},{5,4},{6,7},{7,6},{8,9},{9,8},{10,11... | collective-permute-start | bytes 1572872 | tf_op jit(solution)/shard_map/ppermute | solution.py:260
  31.0 0.1 pad_add_fusion.place_ref
  31.1 0.0 collective-permute-done.3.second
  31.1 0.0 collective-permute-done.swapped
  31.1 1.4 %collective-permute-done.2.passed = bf16[32,8192]{1,0:T(8,128)(2,1)S(1)} collective-permute-done((bf16[32,8192]{1,0:T(8,128)(2,1)S(1)}, bf16[32,8192]{1,0:T(8,128)(2,1)S(1)}, u32[]{:S(2)}, u32[]{:S(2)}) %collective-permute-start.2) | collective-permute-done | bytes 524320 | tf_op jit(solution)/shard_map/ppermute | solution.py:260
  32.5 5.3 %shard_map.56 = bf16[2,2048,128]{2,1,0:T(8,128)(2,1)S(1)} custom-call(s32[3]{0:T(128)S(1)} %pad_add_fusion.place_ref, bf16[32,8192]{1,0:T(8,128)(2,1)S(1)} %get-tuple-element.7.own, bf16[32,8192]{1,0:T(8,128)(2,1)S(1)} %collective-permute-done.swapped, bf16[32,8192]{1,0:T(8,128)(2,1)S(1)} %collective-permute-done.1.first, ...), custom_call_target="tpu_custom_call" | custom-call | tf_op jit(solution)/shard_map/pallas_call | solution.py:159
  37.8 77.2 %all_to_all.10 = bf16[512,8,128]{2,1,0:T(8,128)(2,1)S(1)} all-to-all(bf16[512,8,128]{2,1,0:T(8,128)(2,1)S(1)} %bitcast.8), channel_id=1, replica_groups=mesh['y'=4,'half'=2,'x'=4,'z'=8,'core'=2] {'half','core','x','y','z'}, dimensions={0} | all-to-all | bytes 2097152 | tf_op jit(solution)/shard_map/all_to_all | solution.py:266
  115.0 0.1 copy.8
  115.1 0.3 copy.9
  115.4 1.4 %shard_map.57 = bf16[4,2,4,32,256]{4,3,2,1,0:T(8,128)(2,1)S(1)} custom-call(s32[3]{0:T(128)S(1)} %pad_add_fusion.place_ref, bf16[4,1024,128]{2,1,0:T(8,128)(2,1)S(1)} %bitcast.9), custom_call_target="tpu_custom_call" | custom-call | tf_op jit(solution)/shard_map/pallas_call | solution.py:210
  116.9 12.0 %all_to_all.11.result = bf16[4,2,4,32,256]{4,3,2,1,0:T(8,128)(2,1)S(1)} all-to-all(bf16[4,2,4,32,256]{4,3,2,1,0:T(8,128)(2,1)S(1)} %shard_map.57), channel_id=1, replica_groups=mesh['y'=4,'half'=2,'x'=4,'z'=8,'core'=2] {'y'}, dimensions={0} | all-to-all | bytes 1048576 | tf_op jit(solution)/shard_map/all_to_all | solution.py:270
  128.9 1.0 shard_map.58
Async XLA Ops:
  0.0 22.3 %collective-permute-start.1 = (bf16[32,8192]{1,0:T(8,128)(2,1)}, bf16[32,8192]{1,0:T(8,128)(2,1)S(1)}, u32[]{:S(2)}, u32[]{:S(2)}) collective-permute-start(bf16[32,8192]{1,0:T(8,128)(2,1)} %refs_0_.1), channel_id=1, source_target_pairs={{1,3},{3,5},{5,7},{7,9},{9,11},{11,13},{13,15},{15,17},{17,19},{19... | collective-permute-start | bytes 1572872 | tf_op jit(solution)/shard_map/ppermute | solution.py:256
  4.4 26.7 %collective-permute-start.3 = (bf16[32,8192]{1,0:T(8,128)(2,1)}, bf16[32,8192]{1,0:T(8,128)(2,1)S(1)}, u32[]{:S(2)}, u32[]{:S(2)}) collective-permute-start(bf16[32,8192]{1,0:T(8,128)(2,1)} %refs_0_.1), channel_id=1, source_target_pairs={{0,2},{2,4},{4,6},{6,8},{8,10},{10,12},{12,14},{14,16},{16,18},{18... | collective-permute-start | bytes 1572872 | tf_op jit(solution)/shard_map/ppermute | solution.py:257
  16.6 1.1 copy-start
  17.7 0.9 copy-start.1
  18.8 12.3 %collective-permute-start = (bf16[32,8192]{1,0:T(8,128)(2,1)S(1)}, bf16[32,8192]{1,0:T(8,128)(2,1)S(1)}, u32[]{:S(2)}, u32[]{:S(2)}) collective-permute-start(bf16[32,8192]{1,0:T(8,128)(2,1)S(1)} %get-tuple-element.7.own), channel_id=1, source_target_pairs={{0,1},{1,0},{2,3},{3,2},{4,5},{5,4},{6,7},{7,6},{8,9},{9,8},{10,11... | collective-permute-start | bytes 1572872 | tf_op jit(solution)/shard_map/ppermute | solution.py:259
  22.3 10.2 %collective-permute-start.2 = (bf16[32,8192]{1,0:T(8,128)(2,1)S(1)}, bf16[32,8192]{1,0:T(8,128)(2,1)S(1)}, u32[]{:S(2)}, u32[]{:S(2)}) collective-permute-start(bf16[32,8192]{1,0:T(8,128)(2,1)S(1)} %collective-permute-done.1.first), channel_id=1, source_target_pairs={{0,1},{1,0},{2,3},{3,2},{4,5},{5,4},{6,7},{7,6},{8,9},{9,8},{10,11... | collective-permute-start | bytes 1572872 | tf_op jit(solution)/shard_map/ppermute | solution.py:260

commit v10 on v9

--- a/solution.py
+++ b/solution.py
@@ -119,7 +119,7 @@
                     folded[0, rows, later] = (first - second).astype(jnp.bfloat16)
             return carry
 
-        lax.fori_loop(0, FRAME // 4 // 128, columns, 0)
+        lax.fori_loop(0, FRAME // 4 // 128, columns, 0, unroll=2)
 
     @pl.when(place_ref[1] == 0)
     def _():

time: 130 us -> 130 us (level)
  no operation moved by 1% of the time
where the time goes in v10:
time: 130 us
  blocking collectives  89.2 us (69%)
  starting transfers between devices  28.8 us (22%)
  Pallas kernels  7.88 us (6%)
  local copies, waits for them, and re-layouts  2.37 us (2%)
  waiting for transfers between devices  1.43 us (1%)
    all_to_all x1, blocking collectives, body(): lax.all_to_all(spectra.reshape(devices, CHANNELS * 2, rows), ORDER, 0, 0,...  77.2 us
    ppermute x1, starting transfers between devices, body(): second = lax.ppermute(voltages, TIME, route(up, 0) + route(down, 1))  12.2 us
    all_to_all x1, blocking collectives, body(): result = lax.all_to_all(result, 'y', 0, 0, tiled=True)  12 us
    ppermute x1, starting transfers between devices, body(): passed = lax.ppermute(first, 'core', [(0, 1), (1, 0)])  8.67 us
    pallas_call x1, Pallas kernels, channelize(): pl.pallas_call(channelize_kernel, out_shape=jax.ShapeDtypeStruct((AXES['h...  5.16 us
    ppermute x1, starting transfers between devices, body(): first = lax.ppermute(voltages, TIME, route(up, 1) + route(down, 0))  4.39 us
    ppermute x1, starting transfers between devices, body(): swapped = lax.ppermute(own, 'core', [(0, 1), (1, 0)])  3.5 us
  transfers between devices with their start and end apart: 4, of which 1 were waited for; matrix products, arithmetic and copies ran while one was open for 0% of the time, Pallas kernels for 0%

profile of v10, /device:TPU:1, one launch (start us, length us, event | category | flops | bytes accessed | tf_op | source)
XLA Modules:
  0.0 129.8 jit_solution(4470476451902820617)
XLA Ops:
  0.0 4.4 %collective-permute-start.1 = (bf16[32,8192]{1,0:T(8,128)(2,1)}, bf16[32,8192]{1,0:T(8,128)(2,1)S(1)}, u32[]{:S(2)}, u32[]{:S(2)}) collective-permute-start(bf16[32,8192]{1,0:T(8,128)(2,1)} %refs_0_.1), channel_id=1, source_target_pairs={{1,3},{3,5},{5,7},{7,9},{9,11},{11,13},{13,15},{15,17},{17,19},{19... | collective-permute-start | bytes 1572872 | tf_op jit(solution)/shard_map/ppermute | solution.py:256
  4.4 12.2 %collective-permute-start.3 = (bf16[32,8192]{1,0:T(8,128)(2,1)}, bf16[32,8192]{1,0:T(8,128)(2,1)S(1)}, u32[]{:S(2)}, u32[]{:S(2)}) collective-permute-start(bf16[32,8192]{1,0:T(8,128)(2,1)} %refs_0_.1), channel_id=1, source_target_pairs={{0,2},{2,4},{4,6},{6,8},{8,10},{10,12},{12,14},{14,16},{16,18},{18... | collective-permute-start | bytes 1572872 | tf_op jit(solution)/shard_map/ppermute | solution.py:257
  16.6 0.0 copy-start
  16.6 1.0 copy-done
  17.7 0.0 copy-start.1
  17.7 0.9 copy-done.1
  18.6 0.2 shard_map.55
  18.8 3.5 %collective-permute-start = (bf16[32,8192]{1,0:T(8,128)(2,1)S(1)}, bf16[32,8192]{1,0:T(8,128)(2,1)S(1)}, u32[]{:S(2)}, u32[]{:S(2)}) collective-permute-start(bf16[32,8192]{1,0:T(8,128)(2,1)S(1)} %get-tuple-element.7.own), channel_id=1, source_target_pairs={{0,1},{1,0},{2,3},{3,2},{4,5},{5,4},{6,7},{7,6},{8,9},{9,8},{10,11... | collective-permute-start | bytes 1572872 | tf_op jit(solution)/shard_map/ppermute | solution.py:259
  22.3 0.0 collective-permute-done.1.first
  22.3 8.7 %collective-permute-start.2 = (bf16[32,8192]{1,0:T(8,128)(2,1)S(1)}, bf16[32,8192]{1,0:T(8,128)(2,1)S(1)}, u32[]{:S(2)}, u32[]{:S(2)}) collective-permute-start(bf16[32,8192]{1,0:T(8,128)(2,1)S(1)} %collective-permute-done.1.first), channel_id=1, source_target_pairs={{0,1},{1,0},{2,3},{3,2},{4,5},{5,4},{6,7},{7,6},{8,9},{9,8},{10,11... | collective-permute-start | bytes 1572872 | tf_op jit(solution)/shard_map/ppermute | solution.py:260
  31.0 0.1 pad_add_fusion.place_ref
  31.1 0.0 collective-permute-done.3.second
  31.1 0.0 collective-permute-done.swapped
  31.1 1.4 %collective-permute-done.2.passed = bf16[32,8192]{1,0:T(8,128)(2,1)S(1)} collective-permute-done((bf16[32,8192]{1,0:T(8,128)(2,1)S(1)}, bf16[32,8192]{1,0:T(8,128)(2,1)S(1)}, u32[]{:S(2)}, u32[]{:S(2)}) %collective-permute-start.2) | collective-permute-done | bytes 524320 | tf_op jit(solution)/shard_map/ppermute | solution.py:260
  32.5 5.2 %shard_map.56 = bf16[2,2048,128]{2,1,0:T(8,128)(2,1)S(1)} custom-call(s32[3]{0:T(128)S(1)} %pad_add_fusion.place_ref, bf16[32,8192]{1,0:T(8,128)(2,1)S(1)} %get-tuple-element.7.own, bf16[32,8192]{1,0:T(8,128)(2,1)S(1)} %collective-permute-done.swapped, bf16[32,8192]{1,0:T(8,128)(2,1)S(1)} %collective-permute-done.1.first, ...), custom_call_target="tpu_custom_call" | custom-call | tf_op jit(solution)/shard_map/pallas_call | solution.py:159
  37.7 77.2 %all_to_all.10 = bf16[512,8,128]{2,1,0:T(8,128)(2,1)S(1)} all-to-all(bf16[512,8,128]{2,1,0:T(8,128)(2,1)S(1)} %bitcast.8), channel_id=1, replica_groups=mesh['y'=4,'half'=2,'x'=4,'z'=8,'core'=2] {'half','core','x','y','z'}, dimensions={0} | all-to-all | bytes 2097152 | tf_op jit(solution)/shard_map/all_to_all | solution.py:266
  114.9 0.1 copy.8
  115.0 0.3 copy.9
  115.3 1.5 %shard_map.57 = bf16[4,2,4,32,256]{4,3,2,1,0:T(8,128)(2,1)S(1)} custom-call(s32[3]{0:T(128)S(1)} %pad_add_fusion.place_ref, bf16[4,1024,128]{2,1,0:T(8,128)(2,1)S(1)} %bitcast.9), custom_call_target="tpu_custom_call" | custom-call | tf_op jit(solution)/shard_map/pallas_call | solution.py:210
  116.8 12.0 %all_to_all.11.result = bf16[4,2,4,32,256]{4,3,2,1,0:T(8,128)(2,1)S(1)} all-to-all(bf16[4,2,4,32,256]{4,3,2,1,0:T(8,128)(2,1)S(1)} %shard_map.57), channel_id=1, replica_groups=mesh['y'=4,'half'=2,'x'=4,'z'=8,'core'=2] {'y'}, dimensions={0} | all-to-all | bytes 1048576 | tf_op jit(solution)/shard_map/all_to_all | solution.py:270
  128.7 1.0 shard_map.58
Async XLA Ops:
  0.0 22.3 %collective-permute-start.1 = (bf16[32,8192]{1,0:T(8,128)(2,1)}, bf16[32,8192]{1,0:T(8,128)(2,1)S(1)}, u32[]{:S(2)}, u32[]{:S(2)}) collective-permute-start(bf16[32,8192]{1,0:T(8,128)(2,1)} %refs_0_.1), channel_id=1, source_target_pairs={{1,3},{3,5},{5,7},{7,9},{9,11},{11,13},{13,15},{15,17},{17,19},{19... | collective-permute-start | bytes 1572872 | tf_op jit(solution)/shard_map/ppermute | solution.py:256
  4.4 26.7 %collective-permute-start.3 = (bf16[32,8192]{1,0:T(8,128)(2,1)}, bf16[32,8192]{1,0:T(8,128)(2,1)S(1)}, u32[]{:S(2)}, u32[]{:S(2)}) collective-permute-start(bf16[32,8192]{1,0:T(8,128)(2,1)} %refs_0_.1), channel_id=1, source_target_pairs={{0,2},{2,4},{4,6},{6,8},{8,10},{10,12},{12,14},{14,16},{16,18},{18... | collective-permute-start | bytes 1572872 | tf_op jit(solution)/shard_map/ppermute | solution.py:257
  16.6 1.1 copy-start
  17.7 0.9 copy-start.1
  18.8 12.3 %collective-permute-start = (bf16[32,8192]{1,0:T(8,128)(2,1)S(1)}, bf16[32,8192]{1,0:T(8,128)(2,1)S(1)}, u32[]{:S(2)}, u32[]{:S(2)}) collective-permute-start(bf16[32,8192]{1,0:T(8,128)(2,1)S(1)} %get-tuple-element.7.own), channel_id=1, source_target_pairs={{0,1},{1,0},{2,3},{3,2},{4,5},{5,4},{6,7},{7,6},{8,9},{9,8},{10,11... | collective-permute-start | bytes 1572872 | tf_op jit(solution)/shard_map/ppermute | solution.py:259
  22.3 10.2 %collective-permute-start.2 = (bf16[32,8192]{1,0:T(8,128)(2,1)S(1)}, bf16[32,8192]{1,0:T(8,128)(2,1)S(1)}, u32[]{:S(2)}, u32[]{:S(2)}) collective-permute-start(bf16[32,8192]{1,0:T(8,128)(2,1)S(1)} %collective-permute-done.1.first), channel_id=1, source_target_pairs={{0,1},{1,0},{2,3},{3,2},{4,5},{5,4},{6,7},{7,6},{8,9},{9,8},{10,11... | collective-permute-start | bytes 1572872 | tf_op jit(solution)/shard_map/ppermute | solution.py:260
